TPU v7x, 32 devices: a whole 2x2x4 slice. The times are simulated.
32 devices in a mesh: ctx: 8 (over z, y), tp: 2 (over x), dp: 2 (over core).
Axes of the slice: x: 2, y: 2, z: 4, core: 2. Of those that a mesh axis runs over, the one named last changes fastest.
Arguments:
- vis_qkv: bfloat16 [8192, 3, 1280], P(('dp', 'ctx'), None, 'tp'), parts along dimension 0, may hold values from -60 to 60
- vis_resid: bfloat16 [8192, 1280], P(('dp', 'ctx'), 'tp'), parts along dimension 0, may hold values from -1.796875 to 1.796875
- vis_out_w: bfloat16 [1280, 1280], P(None, 'tp'), may hold values from -0.15625 to 0.15625
- merge_gain: float32 [1280], P('tp'), may hold values from 0.5 to 1.5
- merge_bias: float32 [1280], P('tp'), may hold values from -3 to 3
- vis_kv_w: bfloat16 [4, 1280, 2048], P(None, 'tp'), may hold values from -0.078125 to 0.078125
- frame_host: int32 [16], P('dp'), parts along dimension 0, may hold values from 0 to 7, as said below
- vis_pos: int32 [16], P('dp'), parts along dimension 0, may hold values from 0 to 1920, as said below
- doc_ids: int32 [4096], P('dp'), parts along dimension 0, may hold values from 0 to 3, as said below
- text_kv: bfloat16 [4096, 8, 2, 128], P(('dp', 'ctx'), 'tp'), parts along dimension 0, may hold values from -4 to 4
- queries: bfloat16 [4096, 4096], P(('dp', 'ctx'), 'tp'), parts along dimension 0, may hold values from -50 to 50
Outputs:
- attended: bfloat16 [4096, 4096], P(('dp', 'ctx'), 'tp'), parts along dimension 0
There are 2 independent parts, one for each index of `dp`. A program takes and returns all parts, laid end to end along the dimension named above; an argument that names none is the same for every part. Nothing has to cross between parts.
Inputs may be any that keep to these rules, and one draw needn't show every extreme that they name: `vis_pos`: frame starts are multiples of 128 and increase with the frame; some block of 256 positions holds only frames. `frame_host`: each frame is encoded on the ctx device that holds its positions or on the device 8 / 2 indices away along ctx; every device encodes exactly 1 frame. `doc_ids`: never falls along the sequence.
All inputs are finite; a program needn't handle non-finite values.
Results may differ from a plain program's by a relative error of at most 0.0085.
Values may be sent and summed in bfloat16 or wider, within the bound.
No kernel may reach another device: no remote copies, remote signals or barrier semaphores. Data moves between devices by JAX's collectives and lax.ppermute only.
A program may use at most 64 MiB of HBM per device.

v0:
```python
import math

import jax
import jax.numpy as jnp
from jax import lax
from jax.sharding import PartitionSpec as P

VD = 1280
VH = 16
HD = 128
H = 32
KVH = 8
FT = 128


NEGATIVE = -1e30


def passed_along(block, axis, distance):
    devices = range(lax.axis_size(axis))
    route = [((i - distance) % len(devices), i) for i in devices]
    return lax.ppermute(block, axis, route)


def frame_tables(frame_host, vis_pos, device, per_device, frames_dev):
    count = frame_host.shape[0]
    frame_ids = jnp.arange(count, dtype=jnp.int32)
    earlier = frame_ids[None, :] < frame_ids[:, None]
    same_host = frame_host[:, None] == frame_host[None, :]
    target = vis_pos // per_device
    moving = target != frame_host
    host_rank = jnp.sum(jnp.where(same_host & earlier, 1, 0), axis=1)
    send_rank = jnp.sum(jnp.where(same_host & earlier & moving[None, :], 1, 0), axis=1)
    slot_ids = jnp.arange(frames_dev, dtype=jnp.int32)
    leaving = (frame_host == device) & moving
    send_hit = jnp.any(
        leaving[None, None, :]
        & (send_rank[None, None, :] == slot_ids[:, None, None])
        & (host_rank[None, None, :] == slot_ids[None, :, None]),
        axis=2,
    )
    sending = jnp.where(send_hit, 1.0, 0.0).astype(jnp.bfloat16)
    slot_count = per_device // FT
    arriving = target == device
    local_slot = (vis_pos - device * per_device) // FT
    source = jnp.where(moving, frames_dev + send_rank, host_rank)
    slot_range = jnp.arange(slot_count, dtype=jnp.int32)
    source_range = jnp.arange(2 * frames_dev, dtype=jnp.int32)
    at_slot = arriving[None, :] & (local_slot[None, :] == slot_range[:, None])
    place_hit = jnp.any(
        at_slot[:, None, :] & (source[None, None, :] == source_range[None, :, None]), axis=2
    )
    placing = jnp.where(place_hit, 1.0, 0.0).astype(jnp.bfloat16)
    filled = jnp.any(at_slot, axis=1)
    return (sending, placing, filled)


def shards(
    vis_qkv,
    vis_resid,
    vis_out_w,
    merge_gain,
    merge_bias,
    vis_kv_w,
    frame_host,
    vis_pos,
    doc_ids,
    text_kv,
    queries,
):
    device = lax.axis_index("ctx")
    peers = lax.axis_size("ctx")
    per_device = queries.shape[0]
    patches = vis_qkv.shape[0]
    frames_dev = patches // (4 * FT)
    local_width = vis_qkv.shape[2]
    head_dim = VD // VH
    local_heads = local_width // head_dim
    grouped = vis_qkv.reshape(frames_dev, 4 * FT, 3, local_heads, head_dim)
    vit_scores = jnp.einsum(
        "fqhd,fkhd->fhqk", grouped[:, :, 0], grouped[:, :, 1], preferred_element_type=jnp.float32
    ) / math.sqrt(head_dim)
    vit_max = jnp.max(vit_scores, axis=3, keepdims=True)
    vit_exp = jnp.exp(vit_scores - vit_max)
    vit_total = jnp.sum(vit_exp, axis=3, keepdims=True)
    vit_mixed = jnp.einsum(
        "fhqk,fkhd->fqhd",
        vit_exp.astype(jnp.bfloat16),
        grouped[:, :, 2],
        preferred_element_type=jnp.float32,
    )
    context = (
        (vit_mixed / jnp.transpose(vit_total, (0, 2, 1, 3)))
        .astype(jnp.bfloat16)
        .reshape(patches, local_width)
    )
    hidden = vis_resid.astype(jnp.float32) + jnp.dot(
        lax.all_gather(context, "tp", axis=1, tiled=True),
        vis_out_w,
        preferred_element_type=jnp.float32,
    )
    row_sum, row_squares = lax.psum(
        (jnp.sum(hidden, axis=1), jnp.sum(hidden * hidden, axis=1)), "tp"
    )
    mean_value = row_sum / VD
    variance = row_squares / VD - mean_value * mean_value
    normed = (
        (hidden - mean_value[:, None]) * lax.rsqrt(variance + 1e-06)[:, None] * merge_gain
        + merge_bias
    ).astype(jnp.bfloat16)
    merged = normed.reshape(frames_dev * FT, 4, local_width)
    sending, placing, filled = frame_tables(frame_host, vis_pos, device, per_device, frames_dev)
    local_kv = vis_kv_w.shape[2] // lax.axis_size("tp")
    own_features = merged.reshape(frames_dev, FT * 4 * local_width)
    outgoing = jnp.dot(sending, own_features, preferred_element_type=jnp.float32).astype(
        jnp.bfloat16
    )
    received = passed_along(outgoing, "ctx", peers // 2)
    sources = jnp.concatenate([own_features, received], axis=0)
    arrived_features = jnp.dot(placing, sources, preferred_element_type=jnp.float32)
    arrived_features = arrived_features.astype(jnp.bfloat16).reshape(per_device, 4, local_width)
    arrived = jnp.transpose(
        lax.psum_scatter(
            jnp.einsum(
                "jcr,tjc->rt", vis_kv_w, arrived_features, preferred_element_type=jnp.float32
            ),
            "tp",
            scatter_dimension=0,
            tiled=True,
        )
    ).astype(jnp.bfloat16)
    filled_rows = jnp.repeat(filled, FT)
    kv_heads = local_kv // (2 * HD)
    keys_values = jnp.where(
        filled_rows[:, None], arrived, text_kv.reshape(per_device, local_kv)
    ).reshape(per_device, kv_heads, 2, HD)
    group = H // KVH
    query_rows = queries.reshape(per_device, kv_heads, group, HD)
    first_pos = device * per_device
    last_pos = first_pos + per_device - 1
    query_pos = first_pos + jnp.arange(per_device, dtype=jnp.int32)
    query_doc = lax.dynamic_slice_in_dim(doc_ids, first_pos, per_device)
    score_scale = 1.0 / math.sqrt(HD)
    initial = (
        jnp.full((per_device, kv_heads, group), NEGATIVE, jnp.float32),
        jnp.zeros((per_device, kv_heads, group), jnp.float32),
        jnp.zeros((per_device, kv_heads, group, HD), jnp.float32),
    )
    carry = initial
    key_piece = lax.all_gather(keys_values, "ctx", axis=0, tiled=True)
    row_count = key_piece.shape[0]
    block_rows = math.gcd(row_count, 512)
    block_count = row_count // block_rows
    key_blocks = key_piece.reshape(block_count, block_rows, kv_heads, 2, HD)

    def one_block(softmax_state, packed):
        key_block, block_index = packed
        key_start = block_index * block_rows

        def update(state_in):
            row_max, exp_total, accum = state_in
            key_pos = key_start + jnp.arange(block_rows, dtype=jnp.int32)
            key_doc = lax.dynamic_slice_in_dim(doc_ids, jnp.maximum(key_start, 0), block_rows)
            allowed = (key_pos[None, :] <= query_pos[:, None]) & (
                key_doc[None, :] == query_doc[:, None]
            )
            allowed_full = allowed[:, None, None, :]
            scores = (
                jnp.einsum(
                    "tkgd,skd->tkgs",
                    query_rows,
                    key_block[:, :, 0],
                    preferred_element_type=jnp.float32,
                )
                * score_scale
            )
            new_max = jnp.maximum(
                row_max, jnp.max(jnp.where(allowed_full, scores, NEGATIVE), axis=3)
            )
            exponent = jnp.where(allowed_full, jnp.exp(scores - new_max[..., None]), 0.0)
            factor = jnp.exp(row_max - new_max)
            new_total = exp_total * factor + jnp.sum(exponent, axis=3)
            new_accum = accum * factor[..., None] + jnp.einsum(
                "tkgs,skd->tkgd",
                exponent.astype(jnp.bfloat16),
                key_block[:, :, 1],
                preferred_element_type=jnp.float32,
            )
            return (new_max, new_total, new_accum)

        skipped = (key_start > last_pos) | (key_start < 0)
        return (lax.cond(skipped, lambda unchanged: unchanged, update, softmax_state), None)

    carry, _ = lax.scan(one_block, carry, (key_blocks, jnp.arange(block_count, dtype=jnp.int32)))
    row_max, exp_total, accum = carry
    return (
        (accum / exp_total[..., None])
        .astype(jnp.bfloat16)
        .reshape(per_device, kv_heads * group * HD)
    )


def solution(mesh):
    return jax.shard_map(
        shards,
        mesh=mesh,
        in_specs=(
            P(("dp", "ctx"), None, "tp"),
            P(("dp", "ctx"), "tp"),
            P(None, "tp"),
            P("tp"),
            P("tp"),
            P(None, "tp", None),
            P("dp"),
            P("dp"),
            P("dp"),
            P(("dp", "ctx"), "tp", None, None),
            P(("dp", "ctx"), "tp"),
        ),
        out_specs=P(("dp", "ctx"), "tp"),
        check_vma=False,
    )
```

profile of v0, /device:TPU:25, one launch (start us, length us, event | category | flops | bytes accessed | tf_op | source)
XLA Modules:
  0.0 292.4 jit_solution(10295884706078274315)
XLA Ops:
  6.5 4.1 %copy.27 = bf16[512,3,640]{0,2,1:T(8,128)(2,1)} copy(bf16[512,3,640]{2,0,1:T(8,128)(2,1)} %param.15) | data formatting | bytes 3932160 | tf_op args[0]
  10.7 2.6 multiply_reduce_fusion
  14.7 3.6 %divide_convert_fusion.1 = bf16[1,512,8,80]{1,3,2,0:T(8,128)(2,1)} fusion(f32[8,512,512]{1,2,0:T(8,128)S(1)} %get-tuple-element.221, f32[8,512]{1,0:T(8,128)S(1)} %get-tuple-element.220, bf16[1,512,3,8,80]{1,4,3,2,0:T(8,128)(2,1)} %bitcast.94, f32[512,8]{0,1:T(8,128)S(1)} %bitcast.106), kind=kOutput, calls=%fused_computation.43 | convolution fusion | flops 342491136 | bytes 9732096 | tf_op jit(solution)/shard_map/fhqk,fkhd->fqhd/dot_general | solution.py:86
  19.9 23.7 %all-gather.3.cloned.1.call-done = bf16[512,1280]{0,1:T(8,128)(2,1)} async-done(((bf16[512,640]{0,1:T(8,128)(2,1)}), bf16[512,1280]{0,1:T(8,128)(2,1)}) %all-gather.3.cloned.1.call-update) | async-done | bytes 1310736 | tf_op jit(solution)/shard_map/all_gather | solution.py:98
  43.7 2.8 fusion.40
  46.5 4.0 %all-reduce = (f32[512]{0:T(512)S(1)}, f32[512]{0:T(512)S(1)}) all-reduce(f32[512]{0:T(512)S(1)} %get-tuple-element.181, f32[512]{0:T(512)S(1)} %get-tuple-element.180), channel_id=1, replica_groups=mesh['ctx'=8,'tp'=2,'dp'=2] {'tp'}, use_global_device_ids=true, to_apply=%region_9.10 | all-reduce | flops 1024 | bytes 8192 | tf_op jit(solution)/shard_map/psum | solution.py:102
  53.5 58.2 %collective-permute-done = bf16[1,327680]{1,0:T(2,128)(2,1)} collective-permute-done((bf16[1,327680]{1,0:T(2,128)(2,1)S(1)}, bf16[1,327680]{1,0:T(2,128)(2,1)}, u32[]{:S(2)}, u32[]{:S(2)}) %collective-permute-start) | collective-permute-done | bytes 655392 | tf_op jit(solution)/shard_map/ppermute | solution.py:22
  111.7 4.4 %convolution_convert_fusion = bf16[2,327680]{1,0:T(2,128)(2,1)S(1)} fusion(bf16[1,327680]{1,0:T(2,128)(2,1)} %collective-permute-done, bf16[1,327680]{1,0:T(2,128)(2,1)S(1)} %bitcast.101, pred[2,2]{1,0:T(4,128)(4,1)S(1)} %and_reduce_fusion), kind=kOutput, calls=%fused_computation.25 | convolution fusion | flops 5898248 | bytes 2621444 | tf_op jit(solution)/shard_map/dot_general | solution.py:120
  117.0 7.0 %convolution_bitcast_fusion = f32[2048,256]{0,1:T(8,128)} fusion(bf16[4,640,2048]{2,1,0:T(8,128)(2,1)} %param.20, bf16[256,4,640]{2,1,0:T(4,128)(2,1)S(1)} %reshape.196), kind=kOutput, calls=%fused_computation.33 | convolution fusion | flops 2684354560 | bytes 13893632 | tf_op jit(solution)/shard_map/jcr,tjc->rt/dot_general | solution.py:124
  125.4 30.3 %reduce-scatter.2.cloned.1.call-done = f32[1024,256]{0,1:T(8,128)} async-done(((f32[2048,256]{0,1:T(8,128)}), f32[1024,256]{0,1:T(8,128)}) %reduce-scatter.2.cloned.1.call-update) | async-done | bytes 1048592 | tf_op jit(solution)/shard_map/reduce_scatter | solution.py:123
  158.4 1.5 copy.31
  161.3 69.0 %all-gather.5.cloned.1.call-done = bf16[2048,4,2,128]{3,0,2,1:T(8,128)(2,1)} async-done(((bf16[256,4,2,128]{3,0,2,1:T(8,128)(2,1)}), bf16[2048,4,2,128]{3,0,2,1:T(8,128)(2,1)}) %all-gather.5.cloned.1.call-update) | async-done | bytes 4194320 | tf_op jit(solution)/shard_map/all_gather | solution.py:150
  230.4 4.6 %copy.32 = bf16[4,512,4,2,128]{4,1,2,3,0:T(8,128)(2,1)} copy(bf16[4,512,4,2,128]{4,1,0,3,2:T(8,128)(2,1)} %bitcast.95) | data formatting | bytes 8388608
  234.9 1.5 broadcast_in_dim.97
  236.5 44.9 %while.15 = (s32[]{:T(128)}, f32[256,4,4]{0,2,1:T(4,128)S(1)}, f32[256,4,4]{0,2,1:T(4,128)S(1)}, f32[256,4,4,128]{3,0,2,1:T(8,128)}, s32[4]{0:T(128)S(1)}, /*ind...) while((s32[]{:T(128)}, f32[256,4,4]{0,2,1:T(4,128)S(1)}, ...), condition=%wide.region_17.18_spmd.clone, body=%wide.region_12.17_spmd.clone.sunk | while | flops 1098261248 | bytes 51133840 | solution.py:194
  237.7 10.0 %conditional.3 = (f32[256,4,4]{0,2,1:T(4,128)S(1)}, f32[256,4,4]{0,2,1:T(4,128)S(1)}, f32[256,4,4,128]{3,0,2,1:T(8,128)}) conditional(s32[]{:T(128)} %convert_element_type.82, (s32[]{:T(128)}, s32[]{:T(128)}, s32[2048]{0:T(1024)}, s32[256]{0:T(256)S(1)}, bf16[4,512,4,2,128]{4,1,2,3,0:T(8,128)(2,1)}, /*index=5*/s32[]{:T(128)}, ...), branch_computations={%region_13.15_spmd, %region_16.16_spmd} | conditional | flops 1098261248 | bytes 51099756 | solution.py:192
  240.1 1.4 fusion.2
  241.5 1.7 fusion.6
  243.3 3.1 %bitcast_add_fusion = f32[256,4,4,128]{3,0,2,1:T(8,128)S(1)} fusion(f32[256,4,4,128]{3,0,2,1:T(8,128)S(1)} %copy-done.2, f32[4,512,256,4]{2,1,3,0:T(8,128)S(1)} %get-tuple-element.217, f32[256,4,4]{0,2,1:T(4,128)S(1)} %max.7, pred[256,512]{0,1:T(8,128)(4,1)S(1)} %compare_and_fusion, f32[256,4,4]{0,2,1:T(4,128)S(1)} %bitcast.105, ...), kind=kOutput, calls=%fused_computation.13 | convolution fusion | flops 546308096 | bytes 13271040 | tf_op jit(solution)/shard_map/while/body/eval_jaxpr/cond/branch_0_fun/tkgs,skd->tkgd/dot_general | solution.py:183
  249.0 10.0 %conditional.3 = (f32[256,4,4]{0,2,1:T(4,128)S(1)}, f32[256,4,4]{0,2,1:T(4,128)S(1)}, f32[256,4,4,128]{3,0,2,1:T(8,128)}) conditional(s32[]{:T(128)} %convert_element_type.82, (s32[]{:T(128)}, s32[]{:T(128)}, s32[2048]{0:T(1024)}, s32[256]{0:T(256)S(1)}, bf16[4,512,4,2,128]{4,1,2,3,0:T(8,128)(2,1)}, /*index=5*/s32[]{:T(128)}, ...), branch_computations={%region_13.15_spmd, %region_16.16_spmd} | conditional | flops 1098261248 | bytes 51099756 | solution.py:192
  252.7 1.7 fusion.6
  254.5 3.1 %bitcast_add_fusion = f32[256,4,4,128]{3,0,2,1:T(8,128)S(1)} fusion(f32[256,4,4,128]{3,0,2,1:T(8,128)S(1)} %copy-done.2, f32[4,512,256,4]{2,1,3,0:T(8,128)S(1)} %get-tuple-element.217, f32[256,4,4]{0,2,1:T(4,128)S(1)} %max.7, pred[256,512]{0,1:T(8,128)(4,1)S(1)} %compare_and_fusion, f32[256,4,4]{0,2,1:T(4,128)S(1)} %bitcast.105, ...), kind=kOutput, calls=%fused_computation.13 | convolution fusion | flops 546308096 | bytes 13271040 | tf_op jit(solution)/shard_map/while/body/eval_jaxpr/cond/branch_0_fun/tkgs,skd->tkgd/dot_general | solution.py:183
  260.2 10.0 %conditional.3 = (f32[256,4,4]{0,2,1:T(4,128)S(1)}, f32[256,4,4]{0,2,1:T(4,128)S(1)}, f32[256,4,4,128]{3,0,2,1:T(8,128)}) conditional(s32[]{:T(128)} %convert_element_type.82, (s32[]{:T(128)}, s32[]{:T(128)}, s32[2048]{0:T(1024)}, s32[256]{0:T(256)S(1)}, bf16[4,512,4,2,128]{4,1,2,3,0:T(8,128)(2,1)}, /*index=5*/s32[]{:T(128)}, ...), branch_computations={%region_13.15_spmd, %region_16.16_spmd} | conditional | flops 1098261248 | bytes 51099756 | solution.py:192
  262.5 1.4 fusion.2
  263.9 1.7 fusion.6
  265.7 3.1 %bitcast_add_fusion = f32[256,4,4,128]{3,0,2,1:T(8,128)S(1)} fusion(f32[256,4,4,128]{3,0,2,1:T(8,128)S(1)} %copy-done.2, f32[4,512,256,4]{2,1,3,0:T(8,128)S(1)} %get-tuple-element.217, f32[256,4,4]{0,2,1:T(4,128)S(1)} %max.7, pred[256,512]{0,1:T(8,128)(4,1)S(1)} %compare_and_fusion, f32[256,4,4]{0,2,1:T(4,128)S(1)} %bitcast.105, ...), kind=kOutput, calls=%fused_computation.13 | convolution fusion | flops 546308096 | bytes 13271040 | tf_op jit(solution)/shard_map/while/body/eval_jaxpr/cond/branch_0_fun/tkgs,skd->tkgd/dot_general | solution.py:183
  271.4 10.0 %conditional.3 = (f32[256,4,4]{0,2,1:T(4,128)S(1)}, f32[256,4,4]{0,2,1:T(4,128)S(1)}, f32[256,4,4,128]{3,0,2,1:T(8,128)}) conditional(s32[]{:T(128)} %convert_element_type.82, (s32[]{:T(128)}, s32[]{:T(128)}, s32[2048]{0:T(1024)}, s32[256]{0:T(256)S(1)}, bf16[4,512,4,2,128]{4,1,2,3,0:T(8,128)(2,1)}, /*index=5*/s32[]{:T(128)}, ...), branch_computations={%region_13.15_spmd, %region_16.16_spmd} | conditional | flops 1098261248 | bytes 51099756 | solution.py:192
  273.7 1.4 fusion.2
  275.1 1.7 fusion.6
  276.9 3.1 %bitcast_add_fusion = f32[256,4,4,128]{3,0,2,1:T(8,128)S(1)} fusion(f32[256,4,4,128]{3,0,2,1:T(8,128)S(1)} %copy-done.2, f32[4,512,256,4]{2,1,3,0:T(8,128)S(1)} %get-tuple-element.217, f32[256,4,4]{0,2,1:T(4,128)S(1)} %max.7, pred[256,512]{0,1:T(8,128)(4,1)S(1)} %compare_and_fusion, f32[256,4,4]{0,2,1:T(4,128)S(1)} %bitcast.105, ...), kind=kOutput, calls=%fused_computation.13 | convolution fusion | flops 546308096 | bytes 13271040 | tf_op jit(solution)/shard_map/while/body/eval_jaxpr/cond/branch_0_fun/tkgs,skd->tkgd/dot_general | solution.py:183
  281.3 2.1 divide_convert_fusion
  284.2 1.6 reshape.201
  (104 shorter events, 30.8 us)
Async XLA Ops:
  6.5 37.1 %copy-start = (bf16[1280,640]{1,0:T(8,128)(2,1)S(1)}, bf16[1280,640]{1,0:T(8,128)(2,1)}, u32[]{:S(2)}) copy-start(bf16[1280,640]{1,0:T(8,128)(2,1)} %param.17) | copy-start | bytes 4915204
  6.5 37.1 %all-gather.3.cloned.1.call-start = ((), (), s32[]{:S(2)}) async-start(), calls=%async_computation.1 | async-start | bytes 1966080 | tf_op jit(solution)/shard_map/all_gather | solution.py:98
  14.7 3.7 %copy-start.8 = (s32[8]{0:T(128)S(1)}, s32[8]{0:T(128)}, u32[]{:S(2)}) copy-start(s32[8]{0:T(128)} %param.22) | copy-start | bytes 100
  14.7 3.7 %copy-start.5 = (s32[8]{0:T(128)S(1)}, s32[8]{0:T(128)}, u32[]{:S(2)}) copy-start(s32[8]{0:T(128)} %param.21) | copy-start | bytes 100
  18.3 137.5 %reduce-scatter.2.cloned.1.call-start = ((), (), s32[]{:S(2)}) async-start(), calls=%async_computation.2 | async-start | bytes 3145728 | tf_op jit(solution)/shard_map/reduce_scatter | solution.py:123
  19.9 30.6 %copy-start.6 = (f32[640]{0:T(1024)S(1)}, f32[640]{0:T(1024)}, u32[]{:S(2)}) copy-start(f32[640]{0:T(1024)} %param.19) | copy-start | bytes 7684
  19.9 30.6 %copy-start.7 = (f32[640]{0:T(1024)S(1)}, f32[640]{0:T(1024)}, u32[]{:S(2)}) copy-start(f32[640]{0:T(1024)} %param.18) | copy-start | bytes 7684
  51.9 59.8 %collective-permute-start = (bf16[1,327680]{1,0:T(2,128)(2,1)S(1)}, bf16[1,327680]{1,0:T(2,128)(2,1)}, u32[]{:S(2)}, u32[]{:S(2)}) collective-permute-start(bf16[1,327680]{1,0:T(2,128)(2,1)S(1)} %bitcast.100), channel_id=1, source_target_pairs={{16,0},{20,4},{24,8},{28,12},{0,16},{4,20},{8,24},{12,28},{17,1},{... | collective-permute-start | bytes 1966088 | tf_op jit(solution)/shard_map/ppermute | solution.py:22
  123.9 1.0 copy-start.4
  124.0 106.4 %all-gather.5.cloned.1.call-start = ((), (), s32[]{:S(2)}) async-start(), calls=%async_computation.3 | async-start | bytes 4718592 | tf_op jit(solution)/shard_map/all_gather | solution.py:150
  241.5 1.8 copy-start.2
  246.4 1.3 copy-start.3
  252.7 1.8 copy-start.2
  257.6 1.3 copy-start.3
  263.9 1.8 copy-start.2
  268.8 1.3 copy-start.3
  275.1 1.8 copy-start.2
  280.0 1.3 copy-start.3
  281.3 4.5 %copy-start.1 = (bf16[1280,640]{1,0:T(8,128)(2,1)S(1)}, bf16[1280,640]{1,0:T(8,128)(2,1)}, u32[]{:S(2)}) copy-start(bf16[1280,640]{1,0:T(8,128)(2,1)} %param.17) | copy-start | bytes 4915204
Sparse Core Ops, SparseCore 0:
  18.4 25.2 all-gather.2
  124.1 31.6 reduce-scatter.1
  158.5 71.7 all-gather.4
where the time goes:
time: 293 us; the launch traced here: 292 us
  waiting for transfers between devices  181 us (62%)
  matrix products  38.4 us (13%)
  local copies, waits for them, and re-layouts  36.8 us (13%)
  other arithmetic  14.3 us (5%)
  between operations  13.9 us (5%)
  blocking collectives  3.97 us (1%)
  loops' own time  3.02 us (1%)
    all_gather x1, waiting for transfers between devices, shards(): key_piece = lax.all_gather(keys_values, 'ctx', axis=0, tiled=True)  69 us
    ppermute x1, waiting for transfers between devices, passed_along(): return lax.ppermute(block, axis, route)  58.2 us
    reduce_scatter x1, waiting for transfers between devices, shards(): lax.psum_scatter(jnp.einsum('jcr,tjc->rt', vis_kv_w, arrived_features, pr...  30.3 us
    all_gather x1, waiting for transfers between devices, shards(): lax.all_gather(context, 'tp', axis=1, tiled=True)  23.7 us
    unnamed x20, local copies, waits for them, and re-layouts  13.6 us
    dot_general x4, matrix products, update(): jnp.einsum('tkgs,skd->tkgd', exponent.astype(jnp.bfloat16), key_block[:,...  12.4 us
    reduce_sum x4, other arithmetic, update(): new_total = exp_total * factor + jnp.sum(exponent, axis=3)  6.99 us
    dot_general x1, matrix products, shards(): jnp.einsum('jcr,tjc->rt', vis_kv_w, arrived_features, preferred_element_t...  6.95 us
  transfers between devices with their start and end apart: 4, of which 4 were waited for; matrix products, arithmetic and copies ran while one was open for 2% of the time, Pallas kernels for 0%

commit v1 on v0

v1 whole, which is shorter than its diff:
```python
import functools
import math

import jax
import jax.numpy as jnp
from jax import lax
from jax.experimental import pallas as pl
from jax.experimental.pallas import tpu as pltpu
from jax.sharding import PartitionSpec as P

VD = 1280
VH = 16
HD = 128
H = 32
KVH = 8
FT = 128
FP = 4 * FT
GROUP = H // KVH
LANES = 128

MASKED = -1e30
FLOOR = -1e29
TINY = 1e-30
VMEM_LIMIT = 16 * 1024 * 1024
MERGE_VMEM = 52 * 1024 * 1024
LANGUAGE_VMEM = 52 * 1024 * 1024


def contract_last(a, b):
    return lax.dot_general(a, b, (((1,), (1,)), ((), ())), preferred_element_type=jnp.float32)


def shifted(block, axis, distance):
    count = lax.axis_size(axis)
    return lax.ppermute(block, axis, [(i, (i + distance) % count) for i in range(count)])


def to_next_row(block, rows):
    return lax.ppermute(
        block,
        "ctx",
        [(2 * row + side, 2 * ((row + 1) % rows) + side) for row in range(rows) for side in range(2)],
    )


def to_other_side(block, rows):
    return lax.ppermute(
        block, "ctx", [(2 * row + side, 2 * row + 1 - side) for row in range(rows) for side in range(2)]
    )


class Ring:
    def __init__(self, block, rows):
        self.rows = rows
        self.blocks = [block]
        self.start(block)

    def start(self, block):
        self.moving = to_next_row(block, self.rows) if len(self.blocks) < 2 * self.rows - 1 else None
        self.blocks.append(to_other_side(block, self.rows))

    def advance(self, beside):
        if self.moving is None:
            return beside
        held, self.blocks[-1], beside = lax.optimization_barrier(
            (self.moving, self.blocks[-1], beside)
        )
        self.blocks.append(held)
        self.start(held)
        return beside

    def all(self):
        while self.moving is not None:
            self.advance(())
        return self.blocks


def block_sources(device, rows):
    index = jnp.arange(2 * rows, dtype=jnp.int32)
    row = (device // 2 + rows - index // 2) % rows
    return 2 * row + (device % 2 + index) % 2


def vit_kernel(q_ref, k_ref, v_ref, after_ref, o_ref, *, heads, dim):
    width = q_ref.shape[2]
    to_exp = 1.0 / math.sqrt(dim)
    tiles = {}
    for g in range(heads):
        first, last = g * dim, (g + 1) * dim
        low = first // LANES * LANES
        high = min(width, -(-last // LANES) * LANES)
        lane = lax.broadcasted_iota(jnp.int32, (1, high - low), 1) + low
        inside = (lane >= first) & (lane < last)
        keep = jnp.where(inside, 1.0, 0.0).astype(jnp.bfloat16)
        rest = jnp.where(inside, 0.0, 1.0).astype(jnp.bfloat16)
        scores = contract_last(q_ref[0, :, low:high] * keep, k_ref[0, :, low:high])
        row_max = jnp.max(scores, axis=1, keepdims=True)
        weights = jnp.exp((scores - row_max) * to_exp).astype(jnp.bfloat16)
        mixed = jnp.dot(
            weights, v_ref[0, :, low:high] * keep + rest, preferred_element_type=jnp.float32
        )
        spare = 0 if low < first else last - low
        mixed = mixed / mixed[:, spare : spare + 1]
        for at in range(low, high, LANES):
            end = min(at + LANES, high)
            piece = mixed[:, at - low : end - low]
            if at in tiles:
                piece = jnp.where(inside[:, at - low : end - low], piece, tiles[at])
            tiles[at] = piece
    for at, piece in tiles.items():
        o_ref[:, at : at + piece.shape[1]] = piece.astype(o_ref.dtype)


def vit_attention(fields, after, part, part_count):
    _, patches, width = fields.shape
    frames = patches // FP
    rows = FP // part_count
    dim = VD // VH
    heads = width // dim
    return pl.pallas_call(
        functools.partial(vit_kernel, heads=heads, dim=dim),
        grid=(frames,),
        in_specs=[
            pl.BlockSpec((1, rows, width), lambda f: (0, f * part_count + part, 0)),
            pl.BlockSpec((1, FP, width), lambda f: (1, f, 0)),
            pl.BlockSpec((1, FP, width), lambda f: (2, f, 0)),
            pl.BlockSpec(memory_space=pl.ANY),
        ],
        out_specs=pl.BlockSpec((rows, width), lambda f: (f, 0)),
        out_shape=jax.ShapeDtypeStruct((frames * rows, width), jnp.bfloat16),
        compiler_params=pltpu.CompilerParams(vmem_limit_bytes=VMEM_LIMIT),
        cost_estimate=pl.CostEstimate(flops=1024, bytes_accessed=1024, transcendentals=0),
    )(fields, fields, fields, after)


def merge_kernel(block_ref, x_ref, w_ref, o_ref, held_ref, rows_ref, sems, *, step):
    tokens, columns = o_ref.shape
    patches = x_ref.shape[0]
    steps = columns // step

    def weights_in(n):
        source = w_ref.at[:, :, pl.ds(pl.multiple_of(block_ref[0] * columns + n * step, step), step)]
        return pltpu.make_async_copy(source, held_ref.at[n], sems.at[n])

    for n in range(steps):
        weights_in(n).start()
    token = lax.broadcasted_iota(jnp.int32, (tokens, patches), 0)
    patch = lax.broadcasted_iota(jnp.int32, (tokens, patches), 1)
    for j in range(4):
        pick = jnp.where(patch == 4 * token + j, 1.0, 0.0).astype(jnp.bfloat16)
        rows_ref[j] = jnp.dot(pick, x_ref[...], preferred_element_type=jnp.float32).astype(
            jnp.bfloat16
        )
    for n in range(steps):
        weights_in(n).wait()
        total = jnp.zeros((tokens, step), jnp.float32)
        for j in range(4):
            total = total + jnp.dot(
                rows_ref[j], held_ref[n, j], preferred_element_type=jnp.float32
            )
        o_ref[:, n * step : (n + 1) * step] = total.astype(o_ref.dtype)


def merged_columns(normed, weights, block, columns, dtype):
    patches, width = normed.shape
    tokens = patches // 4
    step = min(columns, 256)
    steps = columns // step
    return pl.pallas_call(
        functools.partial(merge_kernel, step=step),
        in_specs=[
            pl.BlockSpec(memory_space=pltpu.SMEM),
            pl.BlockSpec(memory_space=pltpu.VMEM),
            pl.BlockSpec(memory_space=pl.ANY),
        ],
        out_specs=pl.BlockSpec(memory_space=pltpu.VMEM),
        out_shape=jax.ShapeDtypeStruct((tokens, columns), dtype),
        scratch_shapes=[
            pltpu.VMEM((steps, 4, width, step), jnp.bfloat16),
            pltpu.VMEM((4, tokens, width), jnp.bfloat16),
            pltpu.SemaphoreType.DMA((steps,)),
        ],
        compiler_params=pltpu.CompilerParams(vmem_limit_bytes=MERGE_VMEM),
        cost_estimate=pl.CostEstimate(
            flops=2 * tokens * 4 * width * columns,
            bytes_accessed=4 * width * columns * 2 + patches * width * 2,
            transcendentals=0,
        ),
    )(jnp.reshape(block, (1,)), normed, weights)


def attend_kernel(bounds_ref, rank_ref, slot_pos_ref, low_ref, q_ref, *rest, blocks, final):
    block_refs, rest = rest[:blocks], rest[blocks:]
    kv_ref, query_ref, bias_ref, score_ref, max_ref, acc_ref = rest[-6:]
    rows = low_ref.shape[0]
    scale = 1.0 / math.sqrt(HD)
    first_pair, full_first, full_last, last_pair, first_pos = (bounds_ref[i] for i in range(5))
    lane = lax.broadcasted_iota(jnp.int32, (rows, FT), 1)

    for i, block_ref in enumerate(block_refs):
        kv_ref[pl.ds(pl.multiple_of(rank_ref[i] * FT, FT), FT)] = block_ref[...]
    for g in range(GROUP):
        query_ref[g * rows : (g + 1) * rows] = q_ref[:, g * HD : (g + 1) * HD]

    def mask(pair):
        query_pos = first_pos + lax.broadcasted_iota(jnp.int32, (rows, FT), 0)
        for half in range(2):
            key_pos = slot_pos_ref[2 * pair + half] + lane
            allowed = (key_pos <= query_pos) & (key_pos >= low_ref[...])
            bias_ref[pair, :, half * FT : (half + 1) * FT] = jnp.where(allowed, 0.0, MASKED)

    @pl.when(pl.program_id(0) == 0)
    def _():
        pl.loop(first_pair, full_first)(mask)
        pl.loop(full_last, last_pair)(mask)

    max_ref[...] = jnp.full_like(max_ref, FLOOR)

    def score(pair, masked):
        keys = kv_ref[pl.ds(pl.multiple_of(pair * 2 * FT, 2 * FT), 2 * FT), :HD]
        scores = contract_last(query_ref[...], keys) * scale
        if masked:
            scores = scores.reshape(GROUP, rows, 2 * FT) + bias_ref[pair][None]
            scores = scores.reshape(GROUP * rows, 2 * FT)
        score_ref[pair] = scores
        max_ref[...] = jnp.maximum(max_ref[...], jnp.maximum(scores[:, :FT], scores[:, FT:]))

    pl.loop(first_pair, full_first)(functools.partial(score, masked=True))
    pl.loop(full_first, full_last)(functools.partial(score, masked=False))
    pl.loop(full_last, last_pair)(functools.partial(score, masked=True))

    row_max = jnp.max(max_ref[...], axis=1, keepdims=True)
    if final:
        acc_in_ref, log_in_ref, out_ref = rest[:3]
        logs = jnp.concatenate([log_in_ref[0, :, g : g + 1] for g in range(GROUP)], axis=0)
        row_max = jnp.maximum(row_max, logs)
        weight = jnp.broadcast_to(jnp.exp(logs - row_max), (GROUP * rows, HD))
        for g in range(GROUP):
            here = slice(g * rows, (g + 1) * rows)
            acc_ref[here, :HD] = acc_in_ref[:, g * HD : (g + 1) * HD] * weight[here]
        acc_ref[:, HD:] = weight
    else:
        acc_out_ref, log_out_ref = rest[:2]
        acc_ref[...] = jnp.zeros_like(acc_ref)
    max_ref[...] = jnp.broadcast_to(row_max, max_ref.shape)

    @pl.loop(first_pair, last_pair)
    def _(pair):
        values = kv_ref[pl.ds(pl.multiple_of(pair * 2 * FT, 2 * FT), 2 * FT), HD:]
        values = jnp.concatenate([values, jnp.ones_like(values)], axis=1)
        weights = [
            jnp.exp(score_ref[pair, :, half * FT : (half + 1) * FT] - max_ref[...])
            for half in range(2)
        ]
        weights = jnp.concatenate([each.astype(jnp.bfloat16) for each in weights], axis=1)
        acc_ref[...] += jnp.dot(weights, values, preferred_element_type=jnp.float32)

    if final:
        mixed = acc_ref[:, :HD] / acc_ref[:, HD:]
        for g in range(GROUP):
            out_ref[:, g * HD : (g + 1) * HD] = mixed[g * rows : (g + 1) * rows].astype(
                out_ref.dtype
            )
    else:
        total = jnp.maximum(acc_ref[:, HD:], TINY)
        mixed = acc_ref[:, :HD] / total
        logs = max_ref[...] + jnp.log(total)
        packed = jnp.zeros((rows, FT), jnp.float32)
        for g in range(GROUP):
            here = slice(g * rows, (g + 1) * rows)
            acc_out_ref[:, g * HD : (g + 1) * HD] = mixed[here]
            packed = jnp.where(lane == g, logs[here], packed)
        log_out_ref[0] = packed


def attend(queries, blocks, bounds, rank, slot_pos, low, state=None, head_range=None):
    rows = queries.shape[0]
    columns = blocks[0].shape[1]
    slots = len(blocks)
    pairs = slots // 2
    final = head_range is None
    start, stop = (0, columns // (2 * HD)) if final else head_range
    heads = stop - start
    wide = GROUP * HD
    tall = GROUP * rows
    acc_spec = pl.BlockSpec((rows, wide), lambda h, *_: (0, h))
    log_spec = pl.BlockSpec((1, rows, FT), lambda h, *_: (h, 0, 0))
    in_specs = [
        pl.BlockSpec((rows, FT), lambda h, *_: (0, 0)),
        pl.BlockSpec((rows, wide), lambda h, *_: (0, start + h)),
    ] + [pl.BlockSpec((FT, 2 * HD), lambda h, *_: (0, start + h))] * slots
    if final:
        in_specs += [acc_spec, log_spec]
        out_specs = acc_spec
        out_shape = jax.ShapeDtypeStruct((rows, heads * wide), jnp.bfloat16)
    else:
        out_specs = [acc_spec, log_spec]
        out_shape = [
            jax.ShapeDtypeStruct((rows, heads * wide), jnp.float32),
            jax.ShapeDtypeStruct((heads, rows, FT), jnp.float32),
        ]
    grid_spec = pltpu.PrefetchScalarGridSpec(
        num_scalar_prefetch=3,
        grid=(heads,),
        in_specs=in_specs,
        out_specs=out_specs,
        scratch_shapes=[
            pltpu.VMEM((slots * FT, 2 * HD), jnp.bfloat16),
            pltpu.VMEM((tall, HD), jnp.bfloat16),
            pltpu.VMEM((pairs, rows, 2 * FT), jnp.float32),
            pltpu.VMEM((pairs, tall, 2 * FT), jnp.float32),
            pltpu.VMEM((tall, FT), jnp.float32),
            pltpu.VMEM((tall, 2 * HD), jnp.float32),
        ],
    )
    cells = heads * tall * slots * FT
    return pl.pallas_call(
        functools.partial(attend_kernel, blocks=slots, final=final),
        grid_spec=grid_spec,
        out_shape=out_shape,
        compiler_params=pltpu.CompilerParams(vmem_limit_bytes=LANGUAGE_VMEM),
        cost_estimate=pl.CostEstimate(
            flops=6 * cells * HD,
            bytes_accessed=2 * slots * FT * columns + 8 * heads * tall * FT,
            transcendentals=cells,
        ),
    )(bounds, rank, slot_pos, low, queries, *blocks, *(state or ()))


def pair_bounds(slot_pos, first_pos, last_pos, lowest, highest):
    first, second = slot_pos[0::2], slot_pos[1::2] + (FT - 1)
    begin = jnp.sum((second < lowest).astype(jnp.int32))
    end = jnp.maximum(begin, jnp.sum((first <= last_pos).astype(jnp.int32)))
    full_begin = jnp.clip(jnp.sum((first < highest).astype(jnp.int32)), begin, end)
    full_end = jnp.clip(jnp.sum((second <= first_pos).astype(jnp.int32)), full_begin, end)
    return jnp.stack([begin, full_begin, full_end, end, first_pos]).astype(jnp.int32)


def shards(
    vis_qkv,
    vis_resid,
    vis_out_w,
    merge_gain,
    merge_bias,
    vis_kv_w,
    frame_host,
    vis_pos,
    doc_ids,
    text_kv,
    queries,
):
    device = lax.axis_index("ctx")
    tp_index = lax.axis_index("tp")
    tp_size = lax.axis_size("tp")
    per_device = queries.shape[0]
    patches = vis_qkv.shape[0]
    width = vis_qkv.shape[2]
    frames_dev = patches // FP
    local_kv = vis_kv_w.shape[2] // tp_size
    positions = doc_ids.shape[0]
    frames = vis_pos.shape[0]

    peers = lax.axis_size("ctx")
    rows = peers // 2
    first_pos = device * per_device

    fields = jnp.transpose(vis_qkv, (1, 0, 2))
    part_count = 2 if frames_dev == 1 else 1
    part_rows = patches // part_count
    text_low = text_kv[:FT].reshape(FT, local_kv)
    text_high = text_kv[FT:].reshape(FT, local_kv)
    handed = shifted(text_high, "ctx", peers // 2)
    contexts = [vit_attention(fields, text_high, part, part_count) for part in range(part_count)]
    first_frame = jnp.any(vis_pos == first_pos)
    second_frame = jnp.any(vis_pos == first_pos + FT)
    arrived = [
        [shifted(context, "tp", distance) for distance in range(1, tp_size)]
        for context in contexts
    ]

    def out_rows(distance):
        source = lax.rem(tp_index + tp_size - distance, tp_size)
        return lax.dynamic_slice_in_dim(vis_out_w, source * width, width, axis=0)

    hidden_parts = []
    for part in range(part_count):
        hidden = vis_resid[part * part_rows : (part + 1) * part_rows].astype(jnp.float32)
        for distance in range(tp_size):
            block = contexts[part] if distance == 0 else arrived[part][distance - 1]
            hidden = hidden + jnp.dot(
                block, out_rows(distance), preferred_element_type=jnp.float32
            )
        if part == 0:
            handed, hidden = lax.optimization_barrier((handed, hidden))
            text_block = jnp.where(
                first_frame, jnp.where(second_frame, handed, text_high), text_low
            )
            text = Ring(text_block, rows)
        hidden_parts.append(hidden)
    hidden = jnp.concatenate(hidden_parts, axis=0)
    sums = jnp.stack([jnp.sum(hidden, axis=1), jnp.sum(hidden * hidden, axis=1)])
    others = [shifted(sums, "tp", distance) for distance in range(1, tp_size)]
    sums = text.advance(sums)
    row_sum, row_squares = functools.reduce(jnp.add, others, sums)
    mean_value = row_sum / VD
    variance = row_squares / VD - mean_value * mean_value
    normed = (hidden - mean_value[:, None]) * lax.rsqrt(variance + 1e-06)[
        :, None
    ] * merge_gain + merge_bias
    normed = normed.astype(jnp.bfloat16)

    received = []
    for distance in range(1, tp_size):
        block = lax.rem(tp_index + distance, tp_size)
        part = merged_columns(normed, vis_kv_w, block, local_kv, jnp.bfloat16)
        received.append(shifted(part, "tp", distance))
    normed = text.advance(normed)
    own = merged_columns(normed, vis_kv_w, tp_index, local_kv, jnp.float32)
    own = text.advance(own)
    for part in received:
        own = own + part.astype(jnp.float32)
    sources = block_sources(device, rows)
    frame_ids = jnp.arange(frames, dtype=jnp.int32)
    frame_rank = jnp.sum(
        jnp.where(frame_host[None, :] == sources[:, None], frame_ids[None, :], 0), axis=1
    ).astype(jnp.int32)
    slot_start = jnp.arange(positions // FT, dtype=jnp.int32) * FT
    is_text = jnp.all(slot_start[:, None] != vis_pos[None, :], axis=1)
    text_rank = jnp.sum(
        jnp.where(is_text[None, :] & (slot_start[None, :] < slot_start[:, None]), 1, 0), axis=1
    )
    text_ids = jnp.arange(positions // FT - frames, dtype=jnp.int32)
    text_pos = jnp.sum(
        jnp.where(
            is_text[None, :] & (text_rank[None, :] == text_ids[:, None]), slot_start[None, :], 0
        ),
        axis=1,
    ).astype(jnp.int32)
    owner = text_pos // per_device
    handed_on = jnp.all(vis_pos[None, :] // per_device != owner[:, None], axis=1) & (
        text_pos % per_device != 0
    )
    holder = jnp.where(handed_on, (owner + peers // 2) % peers, owner)
    held_rank = jnp.sum(
        jnp.where(holder[None, :] == sources[:, None], text_ids[None, :], 0), axis=1
    ).astype(jnp.int32)
    query_doc = lax.dynamic_slice_in_dim(doc_ids, first_pos, per_device)
    low = jnp.sum((doc_ids[None, :] < query_doc[:, None]).astype(jnp.int32), axis=1)
    lowest = jnp.sum((doc_ids < query_doc[0]).astype(jnp.int32))
    highest = jnp.sum((doc_ids < query_doc[-1]).astype(jnp.int32))
    low = jnp.broadcast_to(low[:, None], (per_device, FT))
    last_pos = first_pos + per_device - 1
    text_bounds = pair_bounds(text_pos, first_pos, last_pos, lowest, highest)
    vision_bounds = pair_bounds(vis_pos, first_pos, last_pos, lowest, highest)

    text_blocks = text.all()
    heads = local_kv // (2 * HD)
    vision = Ring(own.astype(jnp.bfloat16), rows)
    for _ in range(1, rows - 1):
        vision.advance(())
    text_blocks = vision.advance(text_blocks)
    state = attend(
        queries, text_blocks, text_bounds, held_rank, text_pos, low, head_range=(0, heads)
    )
    return attend(queries, vision.all(), vision_bounds, frame_rank, vis_pos, low, state)


def solution(mesh):
    return jax.shard_map(
        shards,
        mesh=mesh,
        in_specs=(
            P(("dp", "ctx"), None, "tp"),
            P(("dp", "ctx"), "tp"),
            P(None, "tp"),
            P("tp"),
            P("tp"),
            P(None, "tp", None),
            P("dp"),
            P("dp"),
            P("dp"),
            P(("dp", "ctx"), "tp", None, None),
            P(("dp", "ctx"), "tp"),
        ),
        out_specs=P(("dp", "ctx"), "tp"),
        check_vma=False,
    )
```

time: 293 us -> 111 us (0.38)
  the two profiles are of different devices: /device:TPU:25 before, /device:TPU:14 now
where the time goes in v1:
time: 111 us; the launch traced here: 112 us
  Pallas kernels  35 us (32%)
  waiting for transfers between devices  23.7 us (21%)
  starting transfers between devices  20.8 us (19%)
  other arithmetic  11.7 us (11%)
  local copies, waits for them, and re-layouts  9 us (8%)
  between operations  6.54 us (6%)
  matrix products  4.79 us (4%)
    pallas_call x2, Pallas kernels, attend(): pl.pallas_call(functools.partial(attend_kernel, blocks=slots, final=final...  23.4 us
    ppermute x6, waiting for transfers between devices, to_next_row(): lax.ppermute(block, 'ctx', [(2 * row + side, 2 * ((row + 1) % rows) + sid...  9.49 us
    ppermute x6, starting transfers between devices, to_next_row(): lax.ppermute(block, 'ctx', [(2 * row + side, 2 * ((row + 1) % rows) + sid...  8.55 us
    ppermute x5, waiting for transfers between devices, shifted(): lax.ppermute(block, axis, [(i, (i + distance) % count) for i in range(cou...  8.12 us
    pallas_call x2, Pallas kernels, merged_columns(): pl.pallas_call(functools.partial(merge_kernel, step=step), in_specs=[pl.B...  7.18 us
    ppermute x8, starting transfers between devices, to_other_side(): lax.ppermute(block, 'ctx', [(2 * row + side, 2 * row + 1 - side) for row...  6.26 us
    ppermute x8, waiting for transfers between devices, to_other_side(): lax.ppermute(block, 'ctx', [(2 * row + side, 2 * row + 1 - side) for row...  6.11 us
    ppermute x5, starting transfers between devices, shifted(): lax.ppermute(block, axis, [(i, (i + distance) % count) for i in range(cou...  6 us
  transfers between devices with their start and end apart: 19, of which 11 were waited for; matrix products, arithmetic and copies ran while one was open for 17% of the time, Pallas kernels for 19%

profile of v1, /device:TPU:14, one launch (start us, length us, event | category | flops | bytes accessed | tf_op | source)
XLA Modules:
  0.0 111.5 jit_solution(13704656306862986139)
XLA Ops:
  0.0 1.5 %fusion.24 = (bf16[128,4,2,128]{3,2,1,0:T(2,128)(2,1)S(1)}, bf16[128,4,2,128]{3,2,1,0:T(2,128)(2,1)S(1)}) fusion(bf16[256,4,2,128]{3,2,1,0:T(2,128)(2,1)} %param.20), kind=kLoop, calls=%fused_computation.81 | loop fusion | bytes 1048576 | tf_op jit(solution)/shard_map/slice | solution.py:371
  1.7 2.7 %collective-permute-start = (bf16[128,1024]{1,0:T(8,128)(2,1)S(1)}, bf16[128,1024]{1,0:T(8,128)(2,1)S(1)}, u32[]{:S(2)}, u32[]{:S(2)}) collective-permute-start(bf16[128,1024]{1,0:T(8,128)(2,1)S(1)} %reshape.171.after_ref), channel_id=1, source_target_pairs={{0,16},{4,20},{8,24},{12,28},{16,0},{20,4},{24,8},{28,12},{1,17},{... | collective-permute-start | bytes 786440 | tf_op jit(solution)/shard_map/ppermute | solution.py:35
  4.4 1.5 %copy-done.1 = bf16[512,3,640]{2,0,1:T(8,128)(2,1)S(1)} copy-done((bf16[512,3,640]{2,0,1:T(8,128)(2,1)S(1)}, bf16[512,3,640]{2,0,1:T(8,128)(2,1)}, u32[]{:S(2)}) %copy-start.1) | copy-done | bytes 1966104
  5.9 2.2 %shard_map.110 = bf16[256,640]{1,0:T(8,128)(2,1)S(1)} custom-call(bf16[3,512,640]{2,1,0:T(8,128)(2,1)S(1)} %bitcast.22, bf16[3,512,640]{2,1,0:T(8,128)(2,1)S(1)} %bitcast.23, bf16[3,512,640]{2,1,0:T(8,128)(2,1)S(1)} %bitcast.24, bf16[128,1024]{1,0:T(8,128)(2,1)S(1)} %reshape.171.after_ref), custom_call_target="tpu_custom_call" | custom-call | flops 1024 | bytes 1024 | tf_op jit(solution)/shard_map/pallas_call | solution.py:120
  8.7 2.2 %shard_map.109 = bf16[256,640]{1,0:T(8,128)(2,1)S(1)} custom-call(bf16[3,512,640]{2,1,0:T(8,128)(2,1)S(1)} %bitcast.25, bf16[3,512,640]{2,1,0:T(8,128)(2,1)S(1)} %bitcast.26, bf16[3,512,640]{2,1,0:T(8,128)(2,1)S(1)} %bitcast.27, bf16[128,1024]{1,0:T(8,128)(2,1)S(1)} %reshape.171.after_ref), custom_call_target="tpu_custom_call" | custom-call | flops 1024 | bytes 1024 | tf_op jit(solution)/shard_map/pallas_call | solution.py:120
  10.9 1.6 %collective-permute-start.1 = (bf16[256,640]{1,0:T(8,128)(2,1)S(1)}, bf16[256,640]{1,0:T(8,128)(2,1)}, u32[]{:S(2)}, u32[]{:S(2)}) collective-permute-start(bf16[256,640]{1,0:T(8,128)(2,1)S(1)} %shard_map.109), channel_id=1, source_target_pairs={{0,2},{2,0},{1,3},{3,1},{4,6},{6,4},{5,7},{7,5},{8,10},{10,8},{9,1... | collective-permute-start | bytes 983048 | tf_op jit(solution)/shard_map/ppermute | solution.py:35
  13.7 1.5 %convolution_add_fusion.1 = f32[256,640]{1,0:T(8,128)S(1)} fusion(bf16[256,640]{1,0:T(8,128)(2,1)S(1)} %shard_map.110, bf16[1280,640]{1,0:T(8,128)(2,1)S(1)} %copy-done, s32[]{:T(128)S(6)} %select_n.127, bf16[512,640]{1,0:T(8,128)(2,1)} %param.12), kind=kOutput, calls=%fused_computation.5 | convolution fusion | flops 210042880 | bytes 2129924 | tf_op jit(solution)/shard_map/dot_general | solution.py:390
  16.4 8.1 %collective-permute-done.1 = bf16[256,640]{1,0:T(8,128)(2,1)} collective-permute-done((bf16[256,640]{1,0:T(8,128)(2,1)S(1)}, bf16[256,640]{1,0:T(8,128)(2,1)}, u32[]{:S(2)}, u32[]{:S(2)}) %collective-permute-start.1) | collective-permute-done | bytes 327712 | tf_op jit(solution)/shard_map/ppermute | solution.py:35
  24.5 1.4 %convolution_add_fusion.2 = f32[256,640]{1,0:T(8,128)S(1)} fusion(f32[256,640]{1,0:T(8,128)S(1)} %convolution_add_fusion.3, bf16[256,640]{1,0:T(8,128)(2,1)} %collective-permute-done.1, bf16[1280,640]{1,0:T(8,128)(2,1)S(1)} %copy-done, s32[]{:T(128)S(6)} %select_n.128), kind=kOutput, calls=%fused_computation.6 | convolution fusion | flops 209879040 | bytes 2457604 | tf_op jit(solution)/shard_map/dot_general | solution.py:390
  26.6 2.3 %select_select_fusion.rest_0_ = bf16[128,1024]{1,0:T(8,128)(2,1)S(1)} fusion(bf16[128,1024]{1,0:T(8,128)(2,1)S(1)} %reshape.172, bf16[128,1024]{1,0:T(8,128)(2,1)} %copy-done.6, bf16[128,1024]{1,0:T(8,128)(2,1)S(1)} %reshape.171.after_ref, pred[]{:T(512)} %get-tuple-element.70, pred[]{:T(512)} %get-tuple-element.69), kind=kLoop, calls=%fused_computation.14 | loop fusion | flops 262144 | bytes 1048578 | tf_op jit(solution)/shard_map/jit(_where)/select_n | solution.py:395
  29.6 1.4 %convolution_add_fusion = f32[256,640]{1,0:T(8,128)S(1)} fusion(f32[256,640]{1,0:T(8,128)S(1)} %convolution_add_fusion.1, bf16[256,640]{1,0:T(8,128)(2,1)} %collective-permute-done.4, bf16[1280,640]{1,0:T(8,128)(2,1)S(1)} %copy-done, s32[]{:T(128)S(6)} %select_n.128), kind=kOutput, calls=%fused_computation.4 | convolution fusion | flops 209879040 | bytes 2457604 | tf_op jit(solution)/shard_map/dot_general | solution.py:390
  32.5 2.9 %collective-permute-done.2.rest_2_ = bf16[128,1024]{1,0:T(8,128)(2,1)S(1)} collective-permute-done((bf16[128,1024]{1,0:T(8,128)(2,1)S(1)}, bf16[128,1024]{1,0:T(8,128)(2,1)S(1)}, u32[]{:S(2)}, u32[]{:S(2)}) %collective-permute-start.2) | collective-permute-done | bytes 262176 | tf_op jit(solution)/shard_map/ppermute | solution.py:39
  35.5 1.0 collective-permute-start.5
  37.3 3.6 %shard_map.112 = bf16[128,1024]{1,0:T(8,128)(2,1)S(1)} custom-call(s32[1]{0:T(128)} %bitcast.13.block_ref, bf16[512,640]{1,0:T(8,128)(2,1)S(1)} %add_convert_fusion.x_ref, bf16[4,640,2048]{2,1,0:T(8,128)(2,1)} %w_ref.3), custom_call_target="tpu_custom_call" | custom-call | flops 671088640 | bytes 5898240 | tf_op jit(solution)/shard_map/pallas_call | solution.py:169
  42.9 1.5 %collective-permute-start.8 = (bf16[128,1024]{1,0:T(8,128)(2,1)S(1)}, bf16[128,1024]{1,0:T(8,128)(2,1)S(1)}, u32[]{:S(2)}, u32[]{:S(2)}) collective-permute-start(bf16[128,1024]{1,0:T(8,128)(2,1)S(1)} %collective-permute-done.5.rest_4_), channel_id=1, source_target_pairs={{0,8},{4,12},{8,16},{12,20},{16,24},{20,28},{24,0},{28,4},{1,9},{5... | collective-permute-start | bytes 786440 | tf_op jit(solution)/shard_map/ppermute | solution.py:39
  44.9 3.6 %shard_map.111 = f32[128,1024]{1,0:T(8,128)S(1)} custom-call(s32[1]{0:T(128)} %bitcast.12.block_ref, bf16[512,640]{1,0:T(8,128)(2,1)S(1)} %add_convert_fusion.x_ref, bf16[4,640,2048]{2,1,0:T(8,128)(2,1)} %w_ref.3), custom_call_target="tpu_custom_call" | custom-call | flops 671088640 | bytes 5898240 | tf_op jit(solution)/shard_map/pallas_call | solution.py:169
  48.5 1.4 %collective-permute-done.8.rest_6_ = bf16[128,1024]{1,0:T(8,128)(2,1)S(1)} collective-permute-done((bf16[128,1024]{1,0:T(8,128)(2,1)S(1)}, bf16[128,1024]{1,0:T(8,128)(2,1)S(1)}, u32[]{:S(2)}, u32[]{:S(2)}) %collective-permute-start.8) | collective-permute-done | bytes 262176 | tf_op jit(solution)/shard_map/ppermute | solution.py:39
  51.5 2.3 %collective-permute-start.11 = (bf16[128,1024]{1,0:T(8,128)(2,1)S(1)}, bf16[128,1024]{1,0:T(8,128)(2,1)}, u32[]{:S(2)}, u32[]{:S(2)}) collective-permute-start(bf16[128,1024]{1,0:T(8,128)(2,1)S(1)} %add_convert_fusion.1.rest_0_), channel_id=1, source_target_pairs={{0,8},{4,12},{8,16},{12,20},{16,24},{20,28},{24,0},{28,4},{1,9},{5... | collective-permute-start | bytes 786440 | tf_op jit(solution)/shard_map/ppermute | solution.py:39
  54.3 1.9 %convert_reduce_fusion.1 = (s32[]{:T(128)}, s32[]{:T(128)}) fusion(s32[2048]{0:T(1024)S(1)} %copy-done.7, s32[]{:T(128)} %bitcast.2, s32[]{:T(128)} %bitcast), kind=kLoop, calls=%fused_computation.16 | loop fusion | flops 12286 | bytes 8208 | tf_op jit(solution)/shard_map/reduce_sum | solution.py:450
  56.5 1.9 %fusion.10 = (s32[]{:T(128)}, s32[]{:T(128)}, s32[]{:T(128)}, s32[]{:T(128)}) fusion(s32[4]{0:T(128)S(1)} %slice.32, s32[]{:T(128)} %get-tuple-element.61, s32[]{:T(128)S(6)} %sub.47, s32[]{:T(128)} %get-tuple-element.62, s32[]{:T(128)} %mul.59, s32[4]{0:T(128)S(1)} %slice.30), kind=kLoop, calls=%fused_computation.66 | loop fusion | flops 48 | bytes 64 | tf_op jit(solution)/shard_map/reduce_sum | solution.py:334
  58.6 1.2 %collective-permute-done.11.rest_2_ = bf16[128,1024]{1,0:T(8,128)(2,1)} collective-permute-done((bf16[128,1024]{1,0:T(8,128)(2,1)S(1)}, bf16[128,1024]{1,0:T(8,128)(2,1)}, u32[]{:S(2)}, u32[]{:S(2)}) %collective-permute-start.11) | collective-permute-done | bytes 262176 | tf_op jit(solution)/shard_map/ppermute | solution.py:39
  59.8 2.2 %collective-permute-done.12.rest_1_ = bf16[128,1024]{1,0:T(8,128)(2,1)} collective-permute-done((bf16[128,1024]{1,0:T(8,128)(2,1)S(1)}, bf16[128,1024]{1,0:T(8,128)(2,1)}, u32[]{:S(2)}, u32[]{:S(2)}) %collective-permute-start.12) | collective-permute-done | bytes 262176 | tf_op jit(solution)/shard_map/ppermute | solution.py:47
  62.1 1.8 %collective-permute-start.13 = (bf16[128,1024]{1,0:T(8,128)(2,1)}, bf16[128,1024]{1,0:T(8,128)(2,1)}, u32[]{:S(2)}, u32[]{:S(2)}) collective-permute-start(bf16[128,1024]{1,0:T(8,128)(2,1)} %collective-permute-done.11.rest_2_), channel_id=1, source_target_pairs={{0,8},{4,12},{8,16},{12,20},{16,24},{20,28},{24,0},{28,4},{1,9},{5... | collective-permute-start | bytes 786440 | tf_op jit(solution)/shard_map/ppermute | solution.py:39
  64.1 1.3 %fusion.16 = (s32[]{:T(128)}, s32[]{:T(128)}) fusion(s32[4]{0:T(128)S(1)} %slice.38, s32[]{:T(128)} %mul.59, s32[]{:T(128)} %get-tuple-element.62), kind=kLoop, calls=%fused_computation.72 | loop fusion | flops 26 | bytes 32 | tf_op jit(solution)/shard_map/reduce_sum | solution.py:335
  65.5 1.9 %collective-permute-start.17 = (bf16[128,1024]{1,0:T(8,128)(2,1)S(1)}, bf16[128,1024]{1,0:T(8,128)(2,1)}, u32[]{:S(2)}, u32[]{:S(2)}) collective-permute-start(bf16[128,1024]{1,0:T(8,128)(2,1)S(1)} %collective-permute-done.8.rest_6_), channel_id=1, source_target_pairs={{0,4},{4,0},{8,12},{12,8},{16,20},{20,16},{24,28},{28,24},{1,5},{5... | collective-permute-start | bytes 786440 | tf_op jit(solution)/shard_map/ppermute | solution.py:47
  67.4 3.7 %collective-permute-done.13.rest_4_ = bf16[128,1024]{1,0:T(8,128)(2,1)} collective-permute-done((bf16[128,1024]{1,0:T(8,128)(2,1)}, bf16[128,1024]{1,0:T(8,128)(2,1)}, u32[]{:S(2)}, u32[]{:S(2)}) %collective-permute-start.13) | collective-permute-done | bytes 262176 | tf_op jit(solution)/shard_map/ppermute | solution.py:39
  71.0 1.9 %collective-permute-done.14.rest_3_ = bf16[128,1024]{1,0:T(8,128)(2,1)} collective-permute-done((bf16[128,1024]{1,0:T(8,128)(2,1)}, bf16[128,1024]{1,0:T(8,128)(2,1)}, u32[]{:S(2)}, u32[]{:S(2)}) %collective-permute-start.14) | collective-permute-done | bytes 262176 | tf_op jit(solution)/shard_map/ppermute | solution.py:47
  72.9 1.8 %collective-permute-start.15 = (bf16[128,1024]{1,0:T(8,128)(2,1)}, bf16[128,1024]{1,0:T(8,128)(2,1)}, u32[]{:S(2)}, u32[]{:S(2)}) collective-permute-start(bf16[128,1024]{1,0:T(8,128)(2,1)} %collective-permute-done.13.rest_4_), channel_id=1, source_target_pairs={{0,8},{4,12},{8,16},{12,20},{16,24},{20,28},{24,0},{28,4},{1,9},{5... | collective-permute-start | bytes 786440 | tf_op jit(solution)/shard_map/ppermute | solution.py:39
  75.2 1.3 %fusion.15 = (s32[]{:T(128)}, s32[]{:T(128)}) fusion(s32[4]{0:T(128)S(1)} %slice.39, s32[]{:T(128)} %get-tuple-element.61, s32[]{:T(128)S(6)} %sub.47), kind=kLoop, calls=%fused_computation.71 | loop fusion | flops 22 | bytes 32 | tf_op jit(solution)/shard_map/reduce_sum | solution.py:334
  84.8 1.6 %collective-permute-start.18 = (bf16[128,1024]{1,0:T(8,128)(2,1)}, bf16[128,1024]{1,0:T(8,128)(2,1)S(1)}, u32[]{:S(2)}, u32[]{:S(2)}) collective-permute-start(bf16[128,1024]{1,0:T(8,128)(2,1)} %collective-permute-done.15.rest_6_), channel_id=1, source_target_pairs={{0,4},{4,0},{8,12},{12,8},{16,20},{20,16},{24,28},{28,24},{1,5},{5... | collective-permute-start | bytes 786440 | tf_op jit(solution)/shard_map/ppermute | solution.py:47
  87.4 9.7 %shard_map.113 = (f32[256,2048]{1,0:T(8,128)}, f32[4,256,128]{2,1,0:T(8,128)}) custom-call(s32[5]{0:T(128)S(1)} %stack.56.bounds_ref, s32[8]{0:T(128)S(1)} %get-tuple-element.63.rank_ref, s32[8]{0:T(128)S(1)} %select_reduce_fusion.2.slot_pos_ref, s32[256,128]{1,0:T(8,128)S(1)} %broadcast_in_dim.42.low_ref, bf16[256,2048]{1,0:T(8,128)(2,1)} %q_ref.3, ...), custom_call_target="tpu_custom_call" | custom-call | flops 3221225472 | bytes 6291456 | tf_op jit(solution)/shard_map/pallas_call | solution.py:317
  97.9 13.7 %shard_map.114 = bf16[256,2048]{1,0:T(8,128)(2,1)} custom-call(s32[5]{0:T(128)S(1)} %stack.48.bounds_ref, s32[8]{0:T(128)S(1)} %get-tuple-element.64.rank_ref, s32[8]{0:T(128)S(1)} %copy-done.2, s32[256,128]{1,0:T(8,128)S(1)} %broadcast_in_dim.42.low_ref, bf16[256,2048]{1,0:T(8,128)(2,1)} %q_ref.3, bf16[128,1024]{1,0:T(8,128)(2,1)S(1)} %add_convert_fusion.1.rest_0_, ...), custom_call_target="tpu_custom_call" | custom-call | flops 3221225472 | bytes 6291456 | tf_op jit(solution)/shard_map/pallas_call | solution.py:317
  (81 shorter events, 16.3 us)
Async XLA Ops:
  0.0 13.7 %copy-start = (bf16[1280,640]{1,0:T(8,128)(2,1)S(1)}, bf16[1280,640]{1,0:T(8,128)(2,1)}, u32[]{:S(2)}) copy-start(bf16[1280,640]{1,0:T(8,128)(2,1)} %param.13) | copy-start | bytes 4915204
  1.7 24.2 %collective-permute-start = (bf16[128,1024]{1,0:T(8,128)(2,1)S(1)}, bf16[128,1024]{1,0:T(8,128)(2,1)S(1)}, u32[]{:S(2)}, u32[]{:S(2)}) collective-permute-start(bf16[128,1024]{1,0:T(8,128)(2,1)S(1)} %reshape.171.after_ref), channel_id=1, source_target_pairs={{0,16},{4,20},{8,24},{12,28},{16,0},{20,4},{24,8},{28,12},{1,17},{... | collective-permute-start | bytes 786440 | tf_op jit(solution)/shard_map/ppermute | solution.py:35
  4.3 1.5 %copy-start.1 = (bf16[512,3,640]{2,0,1:T(8,128)(2,1)S(1)}, bf16[512,3,640]{2,0,1:T(8,128)(2,1)}, u32[]{:S(2)}) copy-start(bf16[512,3,640]{2,0,1:T(8,128)(2,1)} %param.11) | copy-start | bytes 5898244
  8.1 4.6 %copy-start.2 = (s32[8]{0:T(128)S(1)}, s32[8]{0:T(128)}, u32[]{:S(2)}) copy-start(s32[8]{0:T(128)} %slot_pos_ref.1) | copy-start | bytes 100
  8.1 5.5 %copy-start.7 = (s32[2048]{0:T(1024)S(1)}, s32[2048]{0:T(1024)}, u32[]{:S(2)}) copy-start(s32[2048]{0:T(1024)} %param.19) | copy-start | bytes 24580
  8.1 21.5 %collective-permute-start.4 = (bf16[256,640]{1,0:T(8,128)(2,1)S(1)}, bf16[256,640]{1,0:T(8,128)(2,1)}, u32[]{:S(2)}, u32[]{:S(2)}) collective-permute-start(bf16[256,640]{1,0:T(8,128)(2,1)S(1)} %shard_map.110), channel_id=1, source_target_pairs={{0,2},{2,0},{1,3},{3,1},{4,6},{6,4},{5,7},{7,5},{8,10},{10,8},{9,1... | collective-permute-start | bytes 983048 | tf_op jit(solution)/shard_map/ppermute | solution.py:35
  10.9 13.6 %collective-permute-start.1 = (bf16[256,640]{1,0:T(8,128)(2,1)S(1)}, bf16[256,640]{1,0:T(8,128)(2,1)}, u32[]{:S(2)}, u32[]{:S(2)}) collective-permute-start(bf16[256,640]{1,0:T(8,128)(2,1)S(1)} %shard_map.109), channel_id=1, source_target_pairs={{0,2},{2,0},{1,3},{3,1},{4,6},{6,4},{5,7},{7,5},{8,10},{10,8},{9,1... | collective-permute-start | bytes 983048 | tf_op jit(solution)/shard_map/ppermute | solution.py:35
  13.6 2.3 %copy-start.5 = (bf16[512,640]{1,0:T(8,128)(2,1)S(1)}, bf16[512,640]{1,0:T(8,128)(2,1)}, u32[]{:S(2)}) copy-start(bf16[512,640]{1,0:T(8,128)(2,1)} %param.12) | copy-start | bytes 1966084
  13.7 18.2 %copy-start.8 = (s32[256]{0:T(256)}, s32[256]{0:T(256)S(1)}, u32[]{:S(2)}) copy-start(s32[256]{0:T(256)S(1)} %dynamic_slice.11) | copy-start | bytes 3076
  25.9 0.7 copy-start.6
  28.9 8.1 %copy-start.10 = (f32[640]{0:T(1024)S(1)}, f32[640]{0:T(1024)}, u32[]{:S(2)}) copy-start(f32[640]{0:T(1024)} %param.15) | copy-start | bytes 7684
  28.9 8.1 %copy-start.11 = (f32[640]{0:T(1024)S(1)}, f32[640]{0:T(1024)}, u32[]{:S(2)}) copy-start(f32[640]{0:T(1024)} %param.14) | copy-start | bytes 7684
  29.0 6.4 %collective-permute-start.2 = (bf16[128,1024]{1,0:T(8,128)(2,1)S(1)}, bf16[128,1024]{1,0:T(8,128)(2,1)S(1)}, u32[]{:S(2)}, u32[]{:S(2)}) collective-permute-start(bf16[128,1024]{1,0:T(8,128)(2,1)S(1)} %select_select_fusion.rest_0_), channel_id=1, source_target_pairs={{0,8},{4,12},{8,16},{12,20},{16,24},{20,28},{24,0},{28,4},{1,9},{5... | collective-permute-start | bytes 786440 | tf_op jit(solution)/shard_map/ppermute | solution.py:39
  29.0 6.4 %collective-permute-start.3 = (bf16[128,1024]{1,0:T(8,128)(2,1)S(1)}, bf16[128,1024]{1,0:T(8,128)(2,1)S(1)}, u32[]{:S(2)}, u32[]{:S(2)}) collective-permute-start(bf16[128,1024]{1,0:T(8,128)(2,1)S(1)} %select_select_fusion.rest_0_), channel_id=1, source_target_pairs={{0,4},{4,0},{8,12},{12,8},{16,20},{20,16},{24,28},{28,24},{1,5},{5... | collective-permute-start | bytes 786440 | tf_op jit(solution)/shard_map/ppermute | solution.py:47
  31.3 5.7 %collective-permute-start.7 = (f32[2,512]{1,0:T(2,128)S(1)}, f32[2,512]{1,0:T(2,128)S(1)}, u32[]{:S(2)}, u32[]{:S(2)}) collective-permute-start(f32[2,512]{1,0:T(2,128)S(1)} %pad_maximum_fusion.1), channel_id=1, source_target_pairs={{0,2},{2,0},{1,3},{3,1},{4,6},{6,4},{5,7},{7,5},{8,10},{10,8},{9,1... | collective-permute-start | bytes 12296 | tf_op jit(solution)/shard_map/ppermute | solution.py:35
  35.5 6.4 %collective-permute-start.5 = (bf16[128,1024]{1,0:T(8,128)(2,1)S(1)}, bf16[128,1024]{1,0:T(8,128)(2,1)S(1)}, u32[]{:S(2)}, u32[]{:S(2)}) collective-permute-start(bf16[128,1024]{1,0:T(8,128)(2,1)S(1)} %collective-permute-done.2.rest_2_), channel_id=1, source_target_pairs={{0,8},{4,12},{8,16},{12,20},{16,24},{20,28},{24,0},{28,4},{1,9},{5... | collective-permute-start | bytes 786440 | tf_op jit(solution)/shard_map/ppermute | solution.py:39
  36.5 6.4 %collective-permute-start.6 = (bf16[128,1024]{1,0:T(8,128)(2,1)S(1)}, bf16[128,1024]{1,0:T(8,128)(2,1)S(1)}, u32[]{:S(2)}, u32[]{:S(2)}) collective-permute-start(bf16[128,1024]{1,0:T(8,128)(2,1)S(1)} %collective-permute-done.2.rest_2_), channel_id=1, source_target_pairs={{0,4},{4,0},{8,12},{12,8},{16,20},{20,16},{24,28},{28,24},{1,5},{5... | collective-permute-start | bytes 786440 | tf_op jit(solution)/shard_map/ppermute | solution.py:47
  40.9 9.8 %collective-permute-start.10 = (bf16[128,1024]{1,0:T(8,128)(2,1)S(1)}, bf16[128,1024]{1,0:T(8,128)(2,1)S(1)}, u32[]{:S(2)}, u32[]{:S(2)}) collective-permute-start(bf16[128,1024]{1,0:T(8,128)(2,1)S(1)} %shard_map.112), channel_id=1, source_target_pairs={{0,2},{2,0},{1,3},{3,1},{4,6},{6,4},{5,7},{7,5},{8,10},{10,8},{9,1... | collective-permute-start | bytes 786440 | tf_op jit(solution)/shard_map/ppermute | solution.py:35
  42.9 7.1 %collective-permute-start.8 = (bf16[128,1024]{1,0:T(8,128)(2,1)S(1)}, bf16[128,1024]{1,0:T(8,128)(2,1)S(1)}, u32[]{:S(2)}, u32[]{:S(2)}) collective-permute-start(bf16[128,1024]{1,0:T(8,128)(2,1)S(1)} %collective-permute-done.5.rest_4_), channel_id=1, source_target_pairs={{0,8},{4,12},{8,16},{12,20},{16,24},{20,28},{24,0},{28,4},{1,9},{5... | collective-permute-start | bytes 786440 | tf_op jit(solution)/shard_map/ppermute | solution.py:39
  44.4 6.4 %collective-permute-start.9 = (bf16[128,1024]{1,0:T(8,128)(2,1)S(1)}, bf16[128,1024]{1,0:T(8,128)(2,1)S(1)}, u32[]{:S(2)}, u32[]{:S(2)}) collective-permute-start(bf16[128,1024]{1,0:T(8,128)(2,1)S(1)} %collective-permute-done.5.rest_4_), channel_id=1, source_target_pairs={{0,4},{4,0},{8,12},{12,8},{16,20},{20,16},{24,28},{28,24},{1,5},{5... | collective-permute-start | bytes 786440 | tf_op jit(solution)/shard_map/ppermute | solution.py:47
  44.9 13.5 %copy-start.14 = (s32[8]{0:T(128)S(1)}, s32[8]{0:T(128)}, u32[]{:S(2)}) copy-start(s32[8]{0:T(128)} %and_select_fusion.4) | copy-start | bytes 100
  44.9 39.3 %copy-start.12 = (s32[8]{0:T(128)S(1)}, s32[8]{0:T(128)}, u32[]{:S(2)}) copy-start(s32[8]{0:T(128)} %param.17) | copy-start | bytes 100
  44.9 39.5 %copy-start.9 = (s32[256]{0:T(256)S(1)}, s32[256]{0:T(256)}, u32[]{:S(2)}) copy-start(s32[256]{0:T(256)} %copy-done.8) | copy-start | bytes 3076
  51.5 8.4 %collective-permute-start.11 = (bf16[128,1024]{1,0:T(8,128)(2,1)S(1)}, bf16[128,1024]{1,0:T(8,128)(2,1)}, u32[]{:S(2)}, u32[]{:S(2)}) collective-permute-start(bf16[128,1024]{1,0:T(8,128)(2,1)S(1)} %add_convert_fusion.1.rest_0_), channel_id=1, source_target_pairs={{0,8},{4,12},{8,16},{12,20},{16,24},{20,28},{24,0},{28,4},{1,9},{5... | collective-permute-start | bytes 786440 | tf_op jit(solution)/shard_map/ppermute | solution.py:39
  53.8 8.3 %collective-permute-start.12 = (bf16[128,1024]{1,0:T(8,128)(2,1)S(1)}, bf16[128,1024]{1,0:T(8,128)(2,1)}, u32[]{:S(2)}, u32[]{:S(2)}) collective-permute-start(bf16[128,1024]{1,0:T(8,128)(2,1)S(1)} %add_convert_fusion.1.rest_0_), channel_id=1, source_target_pairs={{0,4},{4,0},{8,12},{12,8},{16,20},{20,16},{24,28},{28,24},{1,5},{5... | collective-permute-start | bytes 786440 | tf_op jit(solution)/shard_map/ppermute | solution.py:47
  62.1 9.0 %collective-permute-start.13 = (bf16[128,1024]{1,0:T(8,128)(2,1)}, bf16[128,1024]{1,0:T(8,128)(2,1)}, u32[]{:S(2)}, u32[]{:S(2)}) collective-permute-start(bf16[128,1024]{1,0:T(8,128)(2,1)} %collective-permute-done.11.rest_2_), channel_id=1, source_target_pairs={{0,8},{4,12},{8,16},{12,20},{16,24},{20,28},{24,0},{28,4},{1,9},{5... | collective-permute-start | bytes 786440 | tf_op jit(solution)/shard_map/ppermute | solution.py:39
  63.9 9.1 %collective-permute-start.14 = (bf16[128,1024]{1,0:T(8,128)(2,1)}, bf16[128,1024]{1,0:T(8,128)(2,1)}, u32[]{:S(2)}, u32[]{:S(2)}) collective-permute-start(bf16[128,1024]{1,0:T(8,128)(2,1)} %collective-permute-done.11.rest_2_), channel_id=1, source_target_pairs={{0,4},{4,0},{8,12},{12,8},{16,20},{20,16},{24,28},{28,24},{1,5},{5... | collective-permute-start | bytes 786440 | tf_op jit(solution)/shard_map/ppermute | solution.py:47
  65.5 19.3 %collective-permute-start.17 = (bf16[128,1024]{1,0:T(8,128)(2,1)S(1)}, bf16[128,1024]{1,0:T(8,128)(2,1)}, u32[]{:S(2)}, u32[]{:S(2)}) collective-permute-start(bf16[128,1024]{1,0:T(8,128)(2,1)S(1)} %collective-permute-done.8.rest_6_), channel_id=1, source_target_pairs={{0,4},{4,0},{8,12},{12,8},{16,20},{20,16},{24,28},{28,24},{1,5},{5... | collective-permute-start | bytes 786440 | tf_op jit(solution)/shard_map/ppermute | solution.py:47
  72.9 11.8 %collective-permute-start.15 = (bf16[128,1024]{1,0:T(8,128)(2,1)}, bf16[128,1024]{1,0:T(8,128)(2,1)}, u32[]{:S(2)}, u32[]{:S(2)}) collective-permute-start(bf16[128,1024]{1,0:T(8,128)(2,1)} %collective-permute-done.13.rest_4_), channel_id=1, source_target_pairs={{0,8},{4,12},{8,16},{12,20},{16,24},{20,28},{24,0},{28,4},{1,9},{5... | collective-permute-start | bytes 786440 | tf_op jit(solution)/shard_map/ppermute | solution.py:39
  74.7 10.0 %collective-permute-start.16 = (bf16[128,1024]{1,0:T(8,128)(2,1)}, bf16[128,1024]{1,0:T(8,128)(2,1)}, u32[]{:S(2)}, u32[]{:S(2)}) collective-permute-start(bf16[128,1024]{1,0:T(8,128)(2,1)} %collective-permute-done.13.rest_4_), channel_id=1, source_target_pairs={{0,4},{4,0},{8,12},{12,8},{16,20},{20,16},{24,28},{28,24},{1,5},{5... | collective-permute-start | bytes 786440 | tf_op jit(solution)/shard_map/ppermute | solution.py:47
  84.8 12.4 %collective-permute-start.18 = (bf16[128,1024]{1,0:T(8,128)(2,1)}, bf16[128,1024]{1,0:T(8,128)(2,1)S(1)}, u32[]{:S(2)}, u32[]{:S(2)}) collective-permute-start(bf16[128,1024]{1,0:T(8,128)(2,1)} %collective-permute-done.15.rest_6_), channel_id=1, source_target_pairs={{0,4},{4,0},{8,12},{12,8},{16,20},{20,16},{24,28},{28,24},{1,5},{5... | collective-permute-start | bytes 786440 | tf_op jit(solution)/shard_map/ppermute | solution.py:47
  86.5 1.0 copy-start.4
  (2 other events, 1.4 us)

commit v2 on v1

--- a/solution.py
+++ b/solution.py
@@ -16,6 +16,7 @@
 FT = 128
 FP = 4 * FT
 GROUP = H // KVH
+DOCS = 4
 LANES = 128
 
 MASKED = -1e30
@@ -73,12 +74,6 @@
         while self.moving is not None:
             self.advance(())
         return self.blocks
-
-
-def block_sources(device, rows):
-    index = jnp.arange(2 * rows, dtype=jnp.int32)
-    row = (device // 2 + rows - index // 2) % rows
-    return 2 * row + (device % 2 + index) % 2
 
 
 def vit_kernel(q_ref, k_ref, v_ref, after_ref, o_ref, *, heads, dim):
@@ -189,151 +184,267 @@
     )(jnp.reshape(block, (1,)), normed, weights)
 
 
-def attend_kernel(bounds_ref, rank_ref, slot_pos_ref, low_ref, q_ref, *rest, blocks, final):
+def tables_kernel(
+    device_ref, vis_pos_ref, frame_host_ref, doc_ref,
+    choice_ref, text_ref, text_rank_ref, text_pos_ref, vision_ref, vision_rank_ref,
+    *, peers, per_device,
+):
+    device = device_ref[0]
+    rows = peers // 2
+    frames, texts = vis_pos_ref.shape[0], text_pos_ref.shape[0]
+    slots_each = per_device // FT
+    first_pos = device * per_device
+    last_pos = first_pos + per_device - 1
+    starts = [
+        jnp.sum(jnp.where(doc_ref[...] < d, 1.0, 0.0)).astype(jnp.int32) for d in range(1, DOCS)
+    ]
+
+    def first_key(pos):
+        return functools.reduce(jnp.maximum, [jnp.where(s <= pos, s, 0) for s in starts])
+
+    lowest, highest = first_key(first_pos), first_key(last_pos)
+
+    def block_from(source):
+        hop = lax.rem(device // 2 + rows - source // 2, rows)
+        return 2 * hop + jnp.where(lax.rem(source, 2) == lax.rem(device, 2), 0, 1)
+
+    def one_frame(f, _):
+        vision_rank_ref[block_from(frame_host_ref[f])] = f
+        return 0
+
+    lax.fori_loop(0, frames, one_frame, 0)
+
+    def one_slot(slot, carry):
+        frame, text, before_is_text, own = carry
+        pos = slot * FT
+        is_frame = (frame < frames) & (vis_pos_ref[jnp.minimum(frame, frames - 1)] == pos)
+        owner = slot // slots_each
+        second = lax.rem(slot, slots_each) != 0
+        partner = lax.rem(owner + peers // 2, peers)
+        holder = jnp.where(second & (before_is_text == 1), partner, owner)
+
+        @pl.when(jnp.logical_not(is_frame))
+        def _():
+            text_pos_ref[text] = pos
+            text_rank_ref[block_from(holder)] = text
+
+        flag = jnp.where(is_frame, 1, 0)
+        own = own + jnp.where(pos == first_pos, flag, 0) + jnp.where(pos == first_pos + FT, 2 * flag, 0)
+        return frame + flag, text + 1 - flag, 1 - flag, own
+
+    zero = jnp.int32(0)
+    _, _, _, own = lax.fori_loop(0, peers * slots_each, one_slot, (zero, zero, zero, zero))
+    choice_ref[0] = jnp.where(own == 3, 2, jnp.where(own == 1, 1, 0))
+
+    for table_ref, pos_ref, count in (
+        (text_ref, text_pos_ref, texts),
+        (vision_ref, vis_pos_ref, frames),
+    ):
+
+        def one_pair(pair, sums):
+            first, last = pos_ref[2 * pair], pos_ref[2 * pair + 1] + FT - 1
+            tests = (last < lowest, first <= last_pos, first < highest, last <= first_pos)
+            return tuple(s + jnp.where(t, 1, 0) for s, t in zip(sums, tests))
+
+        begin, end, full, whole = lax.fori_loop(0, count // 2, one_pair, (zero,) * 4)
+        end = jnp.maximum(begin, end)
+        full = jnp.clip(full, begin, end)
+        whole = jnp.clip(whole, full, end)
+        for i, value in enumerate([begin, full, whole, end, first_pos] + starts):
+            table_ref[i] = value
+
+
+def tables(device, vis_pos, frame_host, doc_ids, peers, per_device):
+    frames = vis_pos.shape[0]
+    texts = doc_ids.shape[0] // FT - frames
+    scalars = pl.BlockSpec(memory_space=pltpu.SMEM)
+    lengths = (1, 4 + DOCS, texts, texts, 4 + DOCS, frames)
+    return pl.pallas_call(
+        functools.partial(tables_kernel, peers=peers, per_device=per_device),
+        in_specs=[scalars] * 3 + [pl.BlockSpec(memory_space=pltpu.VMEM)],
+        out_specs=[scalars] * len(lengths),
+        out_shape=[jax.ShapeDtypeStruct((length,), jnp.int32) for length in lengths],
+    )(jnp.reshape(device, (1,)), vis_pos, frame_host, doc_ids.reshape(-1, LANES))
+
+
+def attend_kernel(
+    table_ref, rank_ref, slot_pos_ref, q_ref, *rest, blocks, rows, final, first_head, heads
+):
     block_refs, rest = rest[:blocks], rest[blocks:]
-    kv_ref, query_ref, bias_ref, score_ref, max_ref, acc_ref = rest[-6:]
-    rows = low_ref.shape[0]
+    if final:
+        acc_refs, log_refs, out_ref = rest[:heads], rest[heads : 2 * heads], rest[2 * heads]
+        held_acc_ref, held_log_ref, result_ref = rest[2 * heads + 1 : 2 * heads + 4]
+    else:
+        acc_out_ref, log_out_ref = rest[:2]
+    kv_ref, held_q_ref, query_ref, bias_ref, score_ref, max_ref, acc_ref, sems = rest[-8:]
     scale = 1.0 / math.sqrt(HD)
-    first_pair, full_first, full_last, last_pair, first_pos = (bounds_ref[i] for i in range(5))
+    wide = GROUP * HD
+    first_pair, full_first, full_last, last_pair, first_pos = (table_ref[i] for i in range(5))
+    starts = [table_ref[i] for i in range(5, 4 + DOCS)]
     lane = lax.broadcasted_iota(jnp.int32, (rows, FT), 1)
 
+    kv_lanes = slice(first_head * 2 * HD, (first_head + heads) * 2 * HD)
+    copies = [
+        (q_ref.at[:, first_head * wide : (first_head + heads) * wide], held_q_ref)
+    ]
     for i, block_ref in enumerate(block_refs):
-        kv_ref[pl.ds(pl.multiple_of(rank_ref[i] * FT, FT), FT)] = block_ref[...]
-    for g in range(GROUP):
-        query_ref[g * rows : (g + 1) * rows] = q_ref[:, g * HD : (g + 1) * HD]
+        there = pl.ds(pl.multiple_of(rank_ref[i] * FT, FT), FT)
+        copies.append((block_ref.at[:, kv_lanes], kv_ref.at[there]))
+    early = len(copies)
+    if final:
+        for h in range(heads):
+            copies += [(acc_refs[h], held_acc_ref.at[h]), (log_refs[h], held_log_ref.at[h])]
+    copies = [pltpu.make_async_copy(*pair, sems.at[i]) for i, pair in enumerate(copies)]
+    for copy in copies:
+        copy.start()
 
     def mask(pair):
         query_pos = first_pos + lax.broadcasted_iota(jnp.int32, (rows, FT), 0)
+        low = functools.reduce(jnp.maximum, [jnp.where(s <= query_pos, s, 0) for s in starts])
         for half in range(2):
             key_pos = slot_pos_ref[2 * pair + half] + lane
-            allowed = (key_pos <= query_pos) & (key_pos >= low_ref[...])
+            allowed = (key_pos <= query_pos) & (key_pos >= low)
             bias_ref[pair, :, half * FT : (half + 1) * FT] = jnp.where(allowed, 0.0, MASKED)
 
-    @pl.when(pl.program_id(0) == 0)
-    def _():
-        pl.loop(first_pair, full_first)(mask)
-        pl.loop(full_last, last_pair)(mask)
-
-    max_ref[...] = jnp.full_like(max_ref, FLOOR)
-
-    def score(pair, masked):
-        keys = kv_ref[pl.ds(pl.multiple_of(pair * 2 * FT, 2 * FT), 2 * FT), :HD]
-        scores = contract_last(query_ref[...], keys) * scale
-        if masked:
-            scores = scores.reshape(GROUP, rows, 2 * FT) + bias_ref[pair][None]
-            scores = scores.reshape(GROUP * rows, 2 * FT)
-        score_ref[pair] = scores
-        max_ref[...] = jnp.maximum(max_ref[...], jnp.maximum(scores[:, :FT], scores[:, FT:]))
-
-    pl.loop(first_pair, full_first)(functools.partial(score, masked=True))
-    pl.loop(full_first, full_last)(functools.partial(score, masked=False))
-    pl.loop(full_last, last_pair)(functools.partial(score, masked=True))
-
-    row_max = jnp.max(max_ref[...], axis=1, keepdims=True)
+    pl.loop(first_pair, full_first)(mask)
+    pl.loop(full_last, last_pair)(mask)
+    for copy in copies[:early]:
+        copy.wait()
+
+    for h in range(heads):
+        for g in range(GROUP):
+            at = h * wide + g * HD
+            query_ref[g * rows : (g + 1) * rows] = held_q_ref[:, at : at + HD]
+        max_ref[...] = jnp.full_like(max_ref, FLOOR)
+
+        def score(pair, masked):
+            here = pl.ds(pl.multiple_of(pair * 2 * FT, 2 * FT), 2 * FT)
+            keys = kv_ref[here, 2 * h * HD : (2 * h + 1) * HD]
+            scores = contract_last(query_ref[...], keys) * scale
+            if masked:
+                scores = scores.reshape(GROUP, rows, 2 * FT) + bias_ref[pair][None]
+                scores = scores.reshape(GROUP * rows, 2 * FT)
+            score_ref[pair] = scores
+            max_ref[...] = jnp.maximum(
+                max_ref[...], jnp.maximum(scores[:, :FT], scores[:, FT:])
+            )
+
+        pl.loop(first_pair, full_first)(functools.partial(score, masked=True))
+        pl.loop(full_first, full_last)(functools.partial(score, masked=False))
+        pl.loop(full_last, last_pair)(functools.partial(score, masked=True))
+
+        row_max = jnp.max(max_ref[...], axis=1, keepdims=True)
+        if final:
+            for copy in copies[early + 2 * h : early + 2 * h + 2]:
+                copy.wait()
+            logs = jnp.concatenate([held_log_ref[h, :, g : g + 1] for g in range(GROUP)], axis=0)
+            row_max = jnp.maximum(row_max, logs)
+            weight = jnp.broadcast_to(jnp.exp(logs - row_max), (GROUP * rows, HD))
+            for g in range(GROUP):
+                here = slice(g * rows, (g + 1) * rows)
+                acc_ref[here, :HD] = held_acc_ref[h, :, g * HD : (g + 1) * HD] * weight[here]
+            acc_ref[:, HD:] = weight
+        else:
+            acc_ref[...] = jnp.zeros_like(acc_ref)
+        max_ref[...] = jnp.broadcast_to(row_max, max_ref.shape)
+
+        @pl.loop(first_pair, last_pair)
+        def _(pair):
+            here = pl.ds(pl.multiple_of(pair * 2 * FT, 2 * FT), 2 * FT)
+            values = kv_ref[here, (2 * h + 1) * HD : (2 * h + 2) * HD]
+            values = jnp.concatenate([values, jnp.ones_like(values)], axis=1)
+            weights = [
+                jnp.exp(score_ref[pair, :, half * FT : (half + 1) * FT] - max_ref[...])
+                for half in range(2)
+            ]
+            weights = jnp.concatenate([each.astype(jnp.bfloat16) for each in weights], axis=1)
+            acc_ref[...] += jnp.dot(weights, values, preferred_element_type=jnp.float32)
+
+        if final:
+            mixed = acc_ref[:, :HD] / acc_ref[:, HD:]
+            for g in range(GROUP):
+                result_ref[h, :, g * HD : (g + 1) * HD] = mixed[
+                    g * rows : (g + 1) * rows
+                ].astype(result_ref.dtype)
+            pltpu.make_async_copy(
+                result_ref.at[h], out_ref.at[:, h * wide : (h + 1) * wide], sems.at[h]
+            ).start()
+        else:
+            total = jnp.maximum(acc_ref[:, HD:], TINY)
+            mixed = acc_ref[:, :HD] / total
+            logs = max_ref[...] + jnp.log(total)
+            packed = jnp.zeros((rows, FT), jnp.float32)
+            for g in range(GROUP):
+                here = slice(g * rows, (g + 1) * rows)
+                acc_out_ref[:, g * HD : (g + 1) * HD] = mixed[here]
+                packed = jnp.where(lane == g, logs[here], packed)
+            log_out_ref[...] = packed
     if final:
-        acc_in_ref, log_in_ref, out_ref = rest[:3]
-        logs = jnp.concatenate([log_in_ref[0, :, g : g + 1] for g in range(GROUP)], axis=0)
-        row_max = jnp.maximum(row_max, logs)
-        weight = jnp.broadcast_to(jnp.exp(logs - row_max), (GROUP * rows, HD))
-        for g in range(GROUP):
-            here = slice(g * rows, (g + 1) * rows)
-            acc_ref[here, :HD] = acc_in_ref[:, g * HD : (g + 1) * HD] * weight[here]
-        acc_ref[:, HD:] = weight
-    else:
-        acc_out_ref, log_out_ref = rest[:2]
-        acc_ref[...] = jnp.zeros_like(acc_ref)
-    max_ref[...] = jnp.broadcast_to(row_max, max_ref.shape)
-
-    @pl.loop(first_pair, last_pair)
-    def _(pair):
-        values = kv_ref[pl.ds(pl.multiple_of(pair * 2 * FT, 2 * FT), 2 * FT), HD:]
-        values = jnp.concatenate([values, jnp.ones_like(values)], axis=1)
-        weights = [
-            jnp.exp(score_ref[pair, :, half * FT : (half + 1) * FT] - max_ref[...])
-            for half in range(2)
-        ]
-        weights = jnp.concatenate([each.astype(jnp.bfloat16) for each in weights], axis=1)
-        acc_ref[...] += jnp.dot(weights, values, preferred_element_type=jnp.float32)
-
-    if final:
-        mixed = acc_ref[:, :HD] / acc_ref[:, HD:]
-        for g in range(GROUP):
-            out_ref[:, g * HD : (g + 1) * HD] = mixed[g * rows : (g + 1) * rows].astype(
-                out_ref.dtype
-            )
-    else:
-        total = jnp.maximum(acc_ref[:, HD:], TINY)
-        mixed = acc_ref[:, :HD] / total
-        logs = max_ref[...] + jnp.log(total)
-        packed = jnp.zeros((rows, FT), jnp.float32)
-        for g in range(GROUP):
-            here = slice(g * rows, (g + 1) * rows)
-            acc_out_ref[:, g * HD : (g + 1) * HD] = mixed[here]
-            packed = jnp.where(lane == g, logs[here], packed)
-        log_out_ref[0] = packed
-
-
-def attend(queries, blocks, bounds, rank, slot_pos, low, state=None, head_range=None):
+        for h in range(heads):
+            pltpu.make_async_copy(
+                result_ref.at[h], out_ref.at[:, h * wide : (h + 1) * wide], sems.at[h]
+            ).wait()
+
+
+def attend(queries, blocks, table, rank, slot_pos, states=None, head=None):
     rows = queries.shape[0]
     columns = blocks[0].shape[1]
     slots = len(blocks)
     pairs = slots // 2
-    final = head_range is None
-    start, stop = (0, columns // (2 * HD)) if final else head_range
-    heads = stop - start
+    final = head is None
+    first_head, heads = (0, columns // (2 * HD)) if final else (head, 1)
     wide = GROUP * HD
     tall = GROUP * rows
-    acc_spec = pl.BlockSpec((rows, wide), lambda h, *_: (0, h))
-    log_spec = pl.BlockSpec((1, rows, FT), lambda h, *_: (h, 0, 0))
-    in_specs = [
-        pl.BlockSpec((rows, FT), lambda h, *_: (0, 0)),
-        pl.BlockSpec((rows, wide), lambda h, *_: (0, start + h)),
-    ] + [pl.BlockSpec((FT, 2 * HD), lambda h, *_: (0, start + h))] * slots
+    anywhere = pl.BlockSpec(memory_space=pl.ANY)
+    whole = pl.BlockSpec(memory_space=pltpu.VMEM)
+    scalars = pl.BlockSpec(memory_space=pltpu.SMEM)
+    scratch = [
+        pltpu.VMEM((slots * FT, heads * 2 * HD), jnp.bfloat16),
+        pltpu.VMEM((rows, heads * wide), jnp.bfloat16),
+        pltpu.VMEM((tall, HD), jnp.bfloat16),
+        pltpu.VMEM((pairs, rows, 2 * FT), jnp.float32),
+        pltpu.VMEM((pairs, tall, 2 * FT), jnp.float32),
+        pltpu.VMEM((tall, FT), jnp.float32),
+        pltpu.VMEM((tall, 2 * HD), jnp.float32),
+        pltpu.SemaphoreType.DMA((1 + slots + 2 * heads,)),
+    ]
+    arrays = []
     if final:
-        in_specs += [acc_spec, log_spec]
-        out_specs = acc_spec
+        arrays = [acc for acc, _ in states] + [logs for _, logs in states]
+        out_specs = anywhere
         out_shape = jax.ShapeDtypeStruct((rows, heads * wide), jnp.bfloat16)
+        scratch = [
+            pltpu.VMEM((heads, rows, wide), jnp.float32),
+            pltpu.VMEM((heads, rows, FT), jnp.float32),
+            pltpu.VMEM((heads, rows, wide), jnp.bfloat16),
+        ] + scratch
     else:
-        out_specs = [acc_spec, log_spec]
+        out_specs = [whole] * 2
         out_shape = [
-            jax.ShapeDtypeStruct((rows, heads * wide), jnp.float32),
-            jax.ShapeDtypeStruct((heads, rows, FT), jnp.float32),
+            jax.ShapeDtypeStruct((rows, wide), jnp.float32),
+            jax.ShapeDtypeStruct((rows, FT), jnp.float32),
         ]
-    grid_spec = pltpu.PrefetchScalarGridSpec(
-        num_scalar_prefetch=3,
-        grid=(heads,),
-        in_specs=in_specs,
-        out_specs=out_specs,
-        scratch_shapes=[
-            pltpu.VMEM((slots * FT, 2 * HD), jnp.bfloat16),
-            pltpu.VMEM((tall, HD), jnp.bfloat16),
-            pltpu.VMEM((pairs, rows, 2 * FT), jnp.float32),
-            pltpu.VMEM((pairs, tall, 2 * FT), jnp.float32),
-            pltpu.VMEM((tall, FT), jnp.float32),
-            pltpu.VMEM((tall, 2 * HD), jnp.float32),
-        ],
-    )
     cells = heads * tall * slots * FT
     return pl.pallas_call(
-        functools.partial(attend_kernel, blocks=slots, final=final),
-        grid_spec=grid_spec,
+        functools.partial(
+            attend_kernel,
+            blocks=slots,
+            rows=rows,
+            final=final,
+            first_head=first_head,
+            heads=heads,
+        ),
+        in_specs=[scalars] * 3 + [anywhere] * (1 + slots + len(arrays)),
+        out_specs=out_specs,
         out_shape=out_shape,
+        scratch_shapes=scratch,
         compiler_params=pltpu.CompilerParams(vmem_limit_bytes=LANGUAGE_VMEM),
         cost_estimate=pl.CostEstimate(
             flops=6 * cells * HD,
             bytes_accessed=2 * slots * FT * columns + 8 * heads * tall * FT,
             transcendentals=cells,
         ),
-    )(bounds, rank, slot_pos, low, queries, *blocks, *(state or ()))
-
-
-def pair_bounds(slot_pos, first_pos, last_pos, lowest, highest):
-    first, second = slot_pos[0::2], slot_pos[1::2] + (FT - 1)
-    begin = jnp.sum((second < lowest).astype(jnp.int32))
-    end = jnp.maximum(begin, jnp.sum((first <= last_pos).astype(jnp.int32)))
-    full_begin = jnp.clip(jnp.sum((first < highest).astype(jnp.int32)), begin, end)
-    full_end = jnp.clip(jnp.sum((second <= first_pos).astype(jnp.int32)), full_begin, end)
-    return jnp.stack([begin, full_begin, full_end, end, first_pos]).astype(jnp.int32)
+    )(table, rank, slot_pos, queries, *blocks, *arrays)
 
 
 def shards(
@@ -370,9 +481,15 @@
     text_low = text_kv[:FT].reshape(FT, local_kv)
     text_high = text_kv[FT:].reshape(FT, local_kv)
     handed = shifted(text_high, "ctx", peers // 2)
-    contexts = [vit_attention(fields, text_high, part, part_count) for part in range(part_count)]
-    first_frame = jnp.any(vis_pos == first_pos)
-    second_frame = jnp.any(vis_pos == first_pos + FT)
+    contexts = []
+    for part in range(part_count):
+        after = text_high if part == 0 else contexts[-1]
+        contexts.append(vit_attention(fields, after, part, part_count))
+    vis_pos_then, _ = lax.optimization_barrier((vis_pos, contexts[-1]))
+    choice, text_table, text_rank, text_pos, vision_table, vision_rank = tables(
+        device, vis_pos_then, frame_host, doc_ids, peers, per_device
+    )
+    choice = choice[0]
     arrived = [
         [shifted(context, "tp", distance) for distance in range(1, tp_size)]
         for context in contexts
@@ -393,7 +510,7 @@
         if part == 0:
             handed, hidden = lax.optimization_barrier((handed, hidden))
             text_block = jnp.where(
-                first_frame, jnp.where(second_frame, handed, text_high), text_low
+                choice == 2, handed, jnp.where(choice == 1, text_high, text_low)
             )
             text = Ring(text_block, rows)
         hidden_parts.append(hidden)
@@ -419,50 +536,25 @@
     own = text.advance(own)
     for part in received:
         own = own + part.astype(jnp.float32)
-    sources = block_sources(device, rows)
-    frame_ids = jnp.arange(frames, dtype=jnp.int32)
-    frame_rank = jnp.sum(
-        jnp.where(frame_host[None, :] == sources[:, None], frame_ids[None, :], 0), axis=1
-    ).astype(jnp.int32)
-    slot_start = jnp.arange(positions // FT, dtype=jnp.int32) * FT
-    is_text = jnp.all(slot_start[:, None] != vis_pos[None, :], axis=1)
-    text_rank = jnp.sum(
-        jnp.where(is_text[None, :] & (slot_start[None, :] < slot_start[:, None]), 1, 0), axis=1
-    )
-    text_ids = jnp.arange(positions // FT - frames, dtype=jnp.int32)
-    text_pos = jnp.sum(
-        jnp.where(
-            is_text[None, :] & (text_rank[None, :] == text_ids[:, None]), slot_start[None, :], 0
-        ),
-        axis=1,
-    ).astype(jnp.int32)
-    owner = text_pos // per_device
-    handed_on = jnp.all(vis_pos[None, :] // per_device != owner[:, None], axis=1) & (
-        text_pos % per_device != 0
-    )
-    holder = jnp.where(handed_on, (owner + peers // 2) % peers, owner)
-    held_rank = jnp.sum(
-        jnp.where(holder[None, :] == sources[:, None], text_ids[None, :], 0), axis=1
-    ).astype(jnp.int32)
-    query_doc = lax.dynamic_slice_in_dim(doc_ids, first_pos, per_device)
-    low = jnp.sum((doc_ids[None, :] < query_doc[:, None]).astype(jnp.int32), axis=1)
-    lowest = jnp.sum((doc_ids < query_doc[0]).astype(jnp.int32))
-    highest = jnp.sum((doc_ids < query_doc[-1]).astype(jnp.int32))
-    low = jnp.broadcast_to(low[:, None], (per_device, FT))
-    last_pos = first_pos + per_device - 1
-    text_bounds = pair_bounds(text_pos, first_pos, last_pos, lowest, highest)
-    vision_bounds = pair_bounds(vis_pos, first_pos, last_pos, lowest, highest)
-
     text_blocks = text.all()
     heads = local_kv // (2 * HD)
     vision = Ring(own.astype(jnp.bfloat16), rows)
-    for _ in range(1, rows - 1):
-        vision.advance(())
-    text_blocks = vision.advance(text_blocks)
-    state = attend(
-        queries, text_blocks, text_bounds, held_rank, text_pos, low, head_range=(0, heads)
-    )
-    return attend(queries, vision.all(), vision_bounds, frame_rank, vis_pos, low, state)
+    states = []
+    for hop in range(1, rows):
+        if hop > 1 and len(states) < heads:
+            states.append(
+                attend(queries, text_blocks, text_table, text_rank, text_pos, head=len(states))
+            )
+            text_blocks, states = vision.advance((text_blocks, states))
+        elif hop == 1:
+            text_blocks = vision.advance(text_blocks)
+        else:
+            vision.advance(())
+    while len(states) < heads:
+        states.append(
+            attend(queries, text_blocks, text_table, text_rank, text_pos, head=len(states))
+        )
+    return attend(queries, vision.all(), vision_table, vision_rank, vis_pos, states)
 
 
 def solution(mesh):

time: 111 us -> 104 us (0.937); the launches traced: 112 us -> 103 us
  other arithmetic: 11.7 us -> 0.69 us
  Pallas kernels: 35 us -> 40.9 us
  between operations: 6.54 us -> 1.76 us
  local copies, waits for them, and re-layouts: 9 us -> 5.78 us
  starting transfers between devices: 20.8 us -> 22.8 us
  waiting for transfers between devices: 23.7 us -> 25.3 us
    reduce_sum x8 -> x0, other arithmetic: 7.18 us -> none  [the longest x2 3.18 us: pair_bounds(): jnp.sum((first < highest).astype(jnp.int32))]
    pallas_call x2 -> x6, Pallas kernels: 23.4 us -> 29.4 us  [the longest x5 27.4 us: attend(): pl.pallas_call(functools.partial(attend_kernel, blocks=slots, rows=rows,...]
    ppermute x8, waiting for transfers between devices: 6.11 us -> 9.94 us  [to_other_side(): lax.ppermute(block, 'ctx', [(2 * row + side, 2 * row + 1 - side) for row...]
    ppermute x5, waiting for transfers between devices: 8.12 us -> 4.55 us  [shifted(): lax.ppermute(block, axis, [(i, (i + distance) % count) for i in range(cou...]
    select_n x4 -> x1, other arithmetic: 2.89 us -> 0.05 us  [shards(): jnp.where(choice == 2, handed, jnp.where(choice == 1, text_high, text_low))]
    unnamed x30 -> x28, local copies, waits for them, and re-layouts: 4.55 us -> 2.28 us
    ppermute x6, starting transfers between devices: 8.55 us -> 10.2 us  [to_next_row(): lax.ppermute(block, 'ctx', [(2 * row + side, 2 * ((row + 1) % rows) + sid...]
    another operation x2 -> x0, local copies, waits for them, and re-layouts: 1.46 us -> none  [pair_bounds(): jnp.stack([begin, full_begin, full_end, end, first_pos]).astype(jnp.int32)]
  transfers between devices with their start and end apart: 19 -> 19, of which waited for: 11 -> 13; matrix products, arithmetic and copies ran while one was open for 17% -> 7% of each run, Pallas kernels for 19% -> 31%
where the time goes in v2:
time: 104 us; the launch traced here: 103 us
  Pallas kernels  40.9 us (39%)
  waiting for transfers between devices  25.3 us (24%)
  starting transfers between devices  22.8 us (22%)
  local copies, waits for them, and re-layouts  5.78 us (6%)
  matrix products  5.73 us (6%)
  between operations  1.76 us (2%)
    pallas_call x5, Pallas kernels, attend(): pl.pallas_call(functools.partial(attend_kernel, blocks=slots, rows=rows,...  27.4 us
    ppermute x6, waiting for transfers between devices, to_next_row(): lax.ppermute(block, 'ctx', [(2 * row + side, 2 * ((row + 1) % rows) + sid...  10.8 us
    ppermute x6, starting transfers between devices, to_next_row(): lax.ppermute(block, 'ctx', [(2 * row + side, 2 * ((row + 1) % rows) + sid...  10.2 us
    ppermute x8, waiting for transfers between devices, to_other_side(): lax.ppermute(block, 'ctx', [(2 * row + side, 2 * row + 1 - side) for row...  9.94 us
    pallas_call x2, Pallas kernels, merged_columns(): pl.pallas_call(functools.partial(merge_kernel, step=step), in_specs=[pl.B...  7.17 us
    ppermute x8, starting transfers between devices, to_other_side(): lax.ppermute(block, 'ctx', [(2 * row + side, 2 * row + 1 - side) for row...  6.55 us
    ppermute x5, starting transfers between devices, shifted(): lax.ppermute(block, axis, [(i, (i + distance) % count) for i in range(cou...  6.01 us
    dot_general x4, matrix products, shards(): jnp.dot(block, out_rows(distance), preferred_element_type=jnp.float32)  5.73 us
  transfers between devices with their start and end apart: 19, of which 13 were waited for; matrix products, arithmetic and copies ran while one was open for 7% of the time, Pallas kernels for 31%

profile of v2, /device:TPU:14, one launch (start us, length us, event | category | flops | bytes accessed | tf_op | source)
XLA Modules:
  0.0 102.9 jit_solution(13620135581575215355)
XLA Ops:
  0.0 2.2 %fusion.9 = (bf16[128,4,2,128]{3,2,1,0:T(2,128)(2,1)}, bf16[128,4,2,128]{3,2,1,0:T(2,128)(2,1)S(1)}) fusion(bf16[256,4,2,128]{3,2,1,0:T(2,128)(2,1)} %param.20), kind=kLoop, calls=%fused_computation.22 | loop fusion | bytes 1048576 | tf_op jit(solution)/shard_map/slice | solution.py:481
  2.4 2.7 %collective-permute-start = (bf16[128,1024]{1,0:T(8,128)(2,1)S(1)}, bf16[128,1024]{1,0:T(8,128)(2,1)}, u32[]{:S(2)}, u32[]{:S(2)}) collective-permute-start(bf16[128,1024]{1,0:T(8,128)(2,1)S(1)} %reshape.46.after_ref), channel_id=1, source_target_pairs={{0,16},{4,20},{8,24},{12,28},{16,0},{20,4},{24,8},{28,12},{1,17},{... | collective-permute-start | bytes 786440 | tf_op jit(solution)/shard_map/ppermute | solution.py:36
  5.0 1.5 %copy-done.1 = bf16[512,3,640]{2,0,1:T(8,128)(2,1)S(1)} copy-done((bf16[512,3,640]{2,0,1:T(8,128)(2,1)S(1)}, bf16[512,3,640]{2,0,1:T(8,128)(2,1)}, u32[]{:S(2)}) %copy-start.1) | copy-done | bytes 1966104
  6.6 2.1 %shard_map.109.after_ref = bf16[256,640]{1,0:T(8,128)(2,1)S(1)} custom-call(bf16[3,512,640]{2,1,0:T(8,128)(2,1)S(1)} %bitcast.15, bf16[3,512,640]{2,1,0:T(8,128)(2,1)S(1)} %bitcast.16, bf16[3,512,640]{2,1,0:T(8,128)(2,1)S(1)} %bitcast.17, bf16[128,1024]{1,0:T(8,128)(2,1)S(1)} %reshape.46.after_ref), custom_call_target="tpu_custom_call" | custom-call | flops 1024 | bytes 1024 | tf_op jit(solution)/shard_map/pallas_call | solution.py:115
  9.3 2.1 %shard_map.110 = bf16[256,640]{1,0:T(8,128)(2,1)S(1)} custom-call(bf16[3,512,640]{2,1,0:T(8,128)(2,1)S(1)} %bitcast.18, bf16[3,512,640]{2,1,0:T(8,128)(2,1)S(1)} %bitcast.19, bf16[3,512,640]{2,1,0:T(8,128)(2,1)S(1)} %bitcast.20, bf16[256,640]{1,0:T(8,128)(2,1)S(1)} %shard_map.109.after_ref), custom_call_target="tpu_custom_call" | custom-call | flops 1024 | bytes 1024 | tf_op jit(solution)/shard_map/pallas_call | solution.py:115
  11.5 1.6 %collective-permute-start.4 = (bf16[256,640]{1,0:T(8,128)(2,1)S(1)}, bf16[256,640]{1,0:T(8,128)(2,1)}, u32[]{:S(2)}, u32[]{:S(2)}) collective-permute-start(bf16[256,640]{1,0:T(8,128)(2,1)S(1)} %shard_map.110), channel_id=1, source_target_pairs={{0,2},{2,0},{1,3},{3,1},{4,6},{6,4},{5,7},{7,5},{8,10},{10,8},{9,1... | collective-permute-start | bytes 983048 | tf_op jit(solution)/shard_map/ppermute | solution.py:36
  14.5 2.1 %shard_map.111 = (s32[1]{0:T(128)}, s32[8]{0:T(128)}, s32[8]{0:T(128)}, s32[8]{0:T(128)}, s32[8]{0:T(128)}, /*index=5*/s32[8]{0:T(128)}) custom-call(s32[1]{0:T(128)} %bitcast.device_ref, s32[8]{0:T(128)} %slot_pos_ref.1, s32[8]{0:T(128)} %frame_host_ref.1, s32[16,128]{1,0:T(8,128)} %bitcast.25), custom_call_target="tpu_custom_call" | custom-call | tf_op jit(solution)/shard_map/pallas_call | solution.py:262
  18.9 1.4 %convolution_add_fusion.3 = f32[256,640]{1,0:T(8,128)S(1)} fusion(bf16[256,640]{1,0:T(8,128)(2,1)S(1)} %shard_map.109.after_ref, bf16[1280,640]{1,0:T(8,128)(2,1)S(1)} %copy-done, s32[]{:T(128)S(6)} %select_n.23, bf16[512,640]{1,0:T(8,128)(2,1)} %param.12), kind=kOutput, calls=%fused_computation.6 | convolution fusion | flops 210042880 | bytes 2129924 | tf_op jit(solution)/shard_map/dot_general | solution.py:507
  20.4 1.4 %convolution_add_fusion.2 = f32[256,640]{1,0:T(8,128)S(1)} fusion(f32[256,640]{1,0:T(8,128)S(1)} %convolution_add_fusion.3, bf16[256,640]{1,0:T(8,128)(2,1)} %collective-permute-done.1, bf16[1280,640]{1,0:T(8,128)(2,1)S(1)} %copy-done, s32[]{:T(128)S(6)} %select_n.24), kind=kOutput, calls=%fused_computation.5 | convolution fusion | flops 209879040 | bytes 2457604 | tf_op jit(solution)/shard_map/dot_general | solution.py:507
  22.8 2.3 %collective-permute-done.4 = bf16[256,640]{1,0:T(8,128)(2,1)} collective-permute-done((bf16[256,640]{1,0:T(8,128)(2,1)S(1)}, bf16[256,640]{1,0:T(8,128)(2,1)}, u32[]{:S(2)}, u32[]{:S(2)}) %collective-permute-start.4) | collective-permute-done | bytes 327712 | tf_op jit(solution)/shard_map/ppermute | solution.py:36
  27.4 1.8 %collective-permute-done.2.rest_2_ = bf16[128,1024]{1,0:T(8,128)(2,1)S(1)} collective-permute-done((bf16[128,1024]{1,0:T(8,128)(2,1)S(1)}, bf16[128,1024]{1,0:T(8,128)(2,1)S(1)}, u32[]{:S(2)}, u32[]{:S(2)}) %collective-permute-start.2) | collective-permute-done | bytes 262176 | tf_op jit(solution)/shard_map/ppermute | solution.py:40
  29.8 1.4 %collective-permute-start.6 = (bf16[128,1024]{1,0:T(8,128)(2,1)S(1)}, bf16[128,1024]{1,0:T(8,128)(2,1)S(1)}, u32[]{:S(2)}, u32[]{:S(2)}) collective-permute-start(bf16[128,1024]{1,0:T(8,128)(2,1)S(1)} %collective-permute-done.2.rest_2_), channel_id=1, source_target_pairs={{0,4},{4,0},{8,12},{12,8},{16,20},{20,16},{24,28},{28,24},{1,5},{5... | collective-permute-start | bytes 786440 | tf_op jit(solution)/shard_map/ppermute | solution.py:48
  31.6 4.4 %collective-permute-done.5.rest_4_ = bf16[128,1024]{1,0:T(8,128)(2,1)S(1)} collective-permute-done((bf16[128,1024]{1,0:T(8,128)(2,1)S(1)}, bf16[128,1024]{1,0:T(8,128)(2,1)S(1)}, u32[]{:S(2)}, u32[]{:S(2)}) %collective-permute-start.5) | collective-permute-done | bytes 262176 | tf_op jit(solution)/shard_map/ppermute | solution.py:40
  36.2 2.5 %collective-permute-start.8 = (bf16[128,1024]{1,0:T(8,128)(2,1)S(1)}, bf16[128,1024]{1,0:T(8,128)(2,1)S(1)}, u32[]{:S(2)}, u32[]{:S(2)}) collective-permute-start(bf16[128,1024]{1,0:T(8,128)(2,1)S(1)} %collective-permute-done.5.rest_4_), channel_id=1, source_target_pairs={{0,8},{4,12},{8,16},{12,20},{16,24},{20,28},{24,0},{28,4},{1,9},{5... | collective-permute-start | bytes 786440 | tf_op jit(solution)/shard_map/ppermute | solution.py:40
  38.7 1.7 %collective-permute-start.9 = (bf16[128,1024]{1,0:T(8,128)(2,1)S(1)}, bf16[128,1024]{1,0:T(8,128)(2,1)S(1)}, u32[]{:S(2)}, u32[]{:S(2)}) collective-permute-start(bf16[128,1024]{1,0:T(8,128)(2,1)S(1)} %collective-permute-done.5.rest_4_), channel_id=1, source_target_pairs={{0,4},{4,0},{8,12},{12,8},{16,20},{20,16},{24,28},{28,24},{1,5},{5... | collective-permute-start | bytes 786440 | tf_op jit(solution)/shard_map/ppermute | solution.py:48
  40.4 3.6 %shard_map.113 = bf16[128,1024]{1,0:T(8,128)(2,1)S(1)} custom-call(s32[1]{0:T(128)} %bitcast.10.block_ref, bf16[512,640]{1,0:T(8,128)(2,1)S(1)} %add_convert_fusion.x_ref, bf16[4,640,2048]{2,1,0:T(8,128)(2,1)} %w_ref.3), custom_call_target="tpu_custom_call" | custom-call | flops 671088640 | bytes 5898240 | tf_op jit(solution)/shard_map/pallas_call | solution.py:164
  44.6 3.6 %shard_map.112 = f32[128,1024]{1,0:T(8,128)S(1)} custom-call(s32[1]{0:T(128)} %bitcast.9.block_ref, bf16[512,640]{1,0:T(8,128)(2,1)S(1)} %add_convert_fusion.x_ref, bf16[4,640,2048]{2,1,0:T(8,128)(2,1)} %w_ref.3), custom_call_target="tpu_custom_call" | custom-call | flops 671088640 | bytes 5898240 | tf_op jit(solution)/shard_map/pallas_call | solution.py:164
  48.2 2.2 %collective-permute-done.10 = bf16[128,1024]{1,0:T(8,128)(2,1)S(1)} collective-permute-done((bf16[128,1024]{1,0:T(8,128)(2,1)S(1)}, bf16[128,1024]{1,0:T(8,128)(2,1)S(1)}, u32[]{:S(2)}, u32[]{:S(2)}) %collective-permute-start.10) | collective-permute-done | bytes 262176 | tf_op jit(solution)/shard_map/ppermute | solution.py:36
  50.5 2.5 %collective-permute-start.11 = (bf16[128,1024]{1,0:T(8,128)(2,1)S(1)}, bf16[128,1024]{1,0:T(8,128)(2,1)S(1)}, u32[]{:S(2)}, u32[]{:S(2)}) collective-permute-start(bf16[128,1024]{1,0:T(8,128)(2,1)S(1)} %add_convert_fusion.1.rest_0_), channel_id=1, source_target_pairs={{0,8},{4,12},{8,16},{12,20},{16,24},{20,28},{24,0},{28,4},{1,9},{5... | collective-permute-start | bytes 786440 | tf_op jit(solution)/shard_map/ppermute | solution.py:40
  53.3 1.7 %collective-permute-start.13 = (bf16[128,1024]{1,0:T(8,128)(2,1)S(1)}, bf16[128,1024]{1,0:T(8,128)(2,1)S(1)}, u32[]{:S(2)}, u32[]{:S(2)}) collective-permute-start(bf16[128,1024]{1,0:T(8,128)(2,1)S(1)} %collective-permute-done.8.rest_6_), channel_id=1, source_target_pairs={{0,4},{4,0},{8,12},{12,8},{16,20},{20,16},{24,28},{28,24},{1,5},{5... | collective-permute-start | bytes 786440 | tf_op jit(solution)/shard_map/ppermute | solution.py:48
  55.0 1.9 %collective-permute-done.11.rest_2_ = bf16[128,1024]{1,0:T(8,128)(2,1)S(1)} collective-permute-done((bf16[128,1024]{1,0:T(8,128)(2,1)S(1)}, bf16[128,1024]{1,0:T(8,128)(2,1)S(1)}, u32[]{:S(2)}, u32[]{:S(2)}) %collective-permute-start.11) | collective-permute-done | bytes 262176 | tf_op jit(solution)/shard_map/ppermute | solution.py:40
  56.9 2.9 %collective-permute-done.12.rest_1_ = bf16[128,1024]{1,0:T(8,128)(2,1)S(1)} collective-permute-done((bf16[128,1024]{1,0:T(8,128)(2,1)S(1)}, bf16[128,1024]{1,0:T(8,128)(2,1)S(1)}, u32[]{:S(2)}, u32[]{:S(2)}) %collective-permute-start.12) | collective-permute-done | bytes 262176 | tf_op jit(solution)/shard_map/ppermute | solution.py:48
  59.9 2.8 %collective-permute-done.13.rest_7_ = bf16[128,1024]{1,0:T(8,128)(2,1)S(1)} collective-permute-done((bf16[128,1024]{1,0:T(8,128)(2,1)S(1)}, bf16[128,1024]{1,0:T(8,128)(2,1)S(1)}, u32[]{:S(2)}, u32[]{:S(2)}) %collective-permute-start.13) | collective-permute-done | bytes 262176 | tf_op jit(solution)/shard_map/ppermute | solution.py:48
  62.7 4.1 %collective-permute-start.14 = (bf16[128,1024]{1,0:T(8,128)(2,1)S(1)}, bf16[128,1024]{1,0:T(8,128)(2,1)S(1)}, u32[]{:S(2)}, u32[]{:S(2)}) collective-permute-start(bf16[128,1024]{1,0:T(8,128)(2,1)S(1)} %collective-permute-done.11.rest_2_), channel_id=1, source_target_pairs={{0,8},{4,12},{8,16},{12,20},{16,24},{20,28},{24,0},{28,4},{1,9},{5... | collective-permute-start | bytes 786440 | tf_op jit(solution)/shard_map/ppermute | solution.py:40
  66.8 4.8 %shard_map.114 = (f32[256,512]{1,0:T(8,128)}, f32[256,128]{1,0:T(8,128)S(1)}) custom-call(s32[8]{0:T(128)S(1)} %copy-done.2, s32[8]{0:T(128)S(1)} %copy-done.3, s32[8]{0:T(128)S(1)} %copy-done.4, bf16[256,2048]{1,0:T(8,128)(2,1)} %q_ref.9, bf16[128,1024]{1,0:T(8,128)(2,1)S(1)} %select_select_fusion.rest_0_, ...), custom_call_target="tpu_custom_call" | custom-call | flops 805306368 | bytes 3145728 | tf_op jit(solution)/shard_map/pallas_call | solution.py:428
  71.7 1.8 %collective-permute-done.14.rest_4_ = bf16[128,1024]{1,0:T(8,128)(2,1)S(1)} collective-permute-done((bf16[128,1024]{1,0:T(8,128)(2,1)S(1)}, bf16[128,1024]{1,0:T(8,128)(2,1)S(1)}, u32[]{:S(2)}, u32[]{:S(2)}) %collective-permute-start.14) | collective-permute-done | bytes 262176 | tf_op jit(solution)/shard_map/ppermute | solution.py:40
  73.4 2.2 %collective-permute-done.15.rest_3_ = bf16[128,1024]{1,0:T(8,128)(2,1)S(1)} collective-permute-done((bf16[128,1024]{1,0:T(8,128)(2,1)S(1)}, bf16[128,1024]{1,0:T(8,128)(2,1)S(1)}, u32[]{:S(2)}, u32[]{:S(2)}) %collective-permute-start.15) | collective-permute-done | bytes 262176 | tf_op jit(solution)/shard_map/ppermute | solution.py:48
  76.3 4.7 %shard_map.115 = (f32[256,512]{1,0:T(8,128)}, f32[256,128]{1,0:T(8,128)S(1)}) custom-call(s32[8]{0:T(128)S(1)} %copy-done.2, s32[8]{0:T(128)S(1)} %copy-done.3, s32[8]{0:T(128)S(1)} %copy-done.4, bf16[256,2048]{1,0:T(8,128)(2,1)} %q_ref.9, bf16[128,1024]{1,0:T(8,128)(2,1)S(1)} %select_select_fusion.rest_0_, ...), custom_call_target="tpu_custom_call" | custom-call | flops 805306368 | bytes 3145728 | tf_op jit(solution)/shard_map/pallas_call | solution.py:428
  82.0 1.7 %collective-permute-done.17.rest_5_ = bf16[128,1024]{1,0:T(8,128)(2,1)S(1)} collective-permute-done((bf16[128,1024]{1,0:T(8,128)(2,1)S(1)}, bf16[128,1024]{1,0:T(8,128)(2,1)S(1)}, u32[]{:S(2)}, u32[]{:S(2)}) %collective-permute-start.17) | collective-permute-done | bytes 262176 | tf_op jit(solution)/shard_map/ppermute | solution.py:48
  84.2 4.7 %shard_map.117 = (f32[256,512]{1,0:T(8,128)}, f32[256,128]{1,0:T(8,128)S(1)}) custom-call(s32[8]{0:T(128)S(1)} %copy-done.2, s32[8]{0:T(128)S(1)} %copy-done.3, s32[8]{0:T(128)S(1)} %copy-done.4, bf16[256,2048]{1,0:T(8,128)(2,1)} %q_ref.9, bf16[128,1024]{1,0:T(8,128)(2,1)S(1)} %select_select_fusion.rest_0_, ...), custom_call_target="tpu_custom_call" | custom-call | flops 805306368 | bytes 3145728 | tf_op jit(solution)/shard_map/pallas_call | solution.py:428
  88.9 4.7 %shard_map.116 = (f32[256,512]{1,0:T(8,128)}, f32[256,128]{1,0:T(8,128)S(1)}) custom-call(s32[8]{0:T(128)S(1)} %copy-done.2, s32[8]{0:T(128)S(1)} %copy-done.3, s32[8]{0:T(128)S(1)} %copy-done.4, bf16[256,2048]{1,0:T(8,128)(2,1)} %q_ref.9, bf16[128,1024]{1,0:T(8,128)(2,1)S(1)} %select_select_fusion.rest_0_, ...), custom_call_target="tpu_custom_call" | custom-call | flops 805306368 | bytes 3145728 | tf_op jit(solution)/shard_map/pallas_call | solution.py:428
  94.3 8.5 %shard_map.118 = bf16[256,2048]{1,0:T(8,128)(2,1)} custom-call(s32[8]{0:T(128)S(1)} %copy-done.6, s32[8]{0:T(128)S(1)} %copy-done.7, s32[8]{0:T(128)S(1)} %copy-done.5, bf16[256,2048]{1,0:T(8,128)(2,1)} %q_ref.9, bf16[128,1024]{1,0:T(8,128)(2,1)S(1)} %add_convert_fusion.1.rest_0_, bf16[128,1024]{1,0:T(8,128)(2,1)S(1)} %collective-permute-done.12.rest_1_, ...), custom_call_target="tpu_custom_call" | custom-call | flops 3221225472 | bytes 6291456 | tf_op jit(solution)/shard_map/pallas_call | solution.py:428
  (59 shorter events, 11.5 us)
Async XLA Ops:
  0.0 13.0 %copy-start = (bf16[1280,640]{1,0:T(8,128)(2,1)S(1)}, bf16[1280,640]{1,0:T(8,128)(2,1)}, u32[]{:S(2)}) copy-start(bf16[1280,640]{1,0:T(8,128)(2,1)} %param.13) | copy-start | bytes 4915204
  2.4 19.5 %collective-permute-start = (bf16[128,1024]{1,0:T(8,128)(2,1)S(1)}, bf16[128,1024]{1,0:T(8,128)(2,1)}, u32[]{:S(2)}, u32[]{:S(2)}) collective-permute-start(bf16[128,1024]{1,0:T(8,128)(2,1)S(1)} %reshape.46.after_ref), channel_id=1, source_target_pairs={{0,16},{4,20},{8,24},{12,28},{16,0},{20,4},{24,8},{28,12},{1,17},{... | collective-permute-start | bytes 786440 | tf_op jit(solution)/shard_map/ppermute | solution.py:36
  5.0 1.5 %copy-start.1 = (bf16[512,3,640]{2,0,1:T(8,128)(2,1)S(1)}, bf16[512,3,640]{2,0,1:T(8,128)(2,1)}, u32[]{:S(2)}) copy-start(bf16[512,3,640]{2,0,1:T(8,128)(2,1)} %param.11) | copy-start | bytes 5898244
  8.7 11.7 %collective-permute-start.1 = (bf16[256,640]{1,0:T(8,128)(2,1)S(1)}, bf16[256,640]{1,0:T(8,128)(2,1)}, u32[]{:S(2)}, u32[]{:S(2)}) collective-permute-start(bf16[256,640]{1,0:T(8,128)(2,1)S(1)} %shard_map.109.after_ref), channel_id=1, source_target_pairs={{0,2},{2,0},{1,3},{3,1},{4,6},{6,4},{5,7},{7,5},{8,10},{10,8},{9,1... | collective-permute-start | bytes 983048 | tf_op jit(solution)/shard_map/ppermute | solution.py:36
  11.5 13.6 %collective-permute-start.4 = (bf16[256,640]{1,0:T(8,128)(2,1)S(1)}, bf16[256,640]{1,0:T(8,128)(2,1)}, u32[]{:S(2)}, u32[]{:S(2)}) collective-permute-start(bf16[256,640]{1,0:T(8,128)(2,1)S(1)} %shard_map.110), channel_id=1, source_target_pairs={{0,2},{2,0},{1,3},{3,1},{4,6},{6,4},{5,7},{7,5},{8,10},{10,8},{9,1... | collective-permute-start | bytes 983048 | tf_op jit(solution)/shard_map/ppermute | solution.py:36
  21.9 9.4 %copy-start.9 = (f32[640]{0:T(1024)S(1)}, f32[640]{0:T(1024)}, u32[]{:S(2)}) copy-start(f32[640]{0:T(1024)} %param.15) | copy-start | bytes 7684
  21.9 9.4 %copy-start.10 = (f32[640]{0:T(1024)S(1)}, f32[640]{0:T(1024)}, u32[]{:S(2)}) copy-start(f32[640]{0:T(1024)} %param.14) | copy-start | bytes 7684
  21.9 7.3 %collective-permute-start.2 = (bf16[128,1024]{1,0:T(8,128)(2,1)S(1)}, bf16[128,1024]{1,0:T(8,128)(2,1)S(1)}, u32[]{:S(2)}, u32[]{:S(2)}) collective-permute-start(bf16[128,1024]{1,0:T(8,128)(2,1)S(1)} %select_select_fusion.rest_0_), channel_id=1, source_target_pairs={{0,8},{4,12},{8,16},{12,20},{16,24},{20,28},{24,0},{28,4},{1,9},{5... | collective-permute-start | bytes 786440 | tf_op jit(solution)/shard_map/ppermute | solution.py:40
  22.2 7.0 %collective-permute-start.3 = (bf16[128,1024]{1,0:T(8,128)(2,1)S(1)}, bf16[128,1024]{1,0:T(8,128)(2,1)S(1)}, u32[]{:S(2)}, u32[]{:S(2)}) collective-permute-start(bf16[128,1024]{1,0:T(8,128)(2,1)S(1)} %select_select_fusion.rest_0_), channel_id=1, source_target_pairs={{0,4},{4,0},{8,12},{12,8},{16,20},{20,16},{24,28},{28,24},{1,5},{5... | collective-permute-start | bytes 786440 | tf_op jit(solution)/shard_map/ppermute | solution.py:48
  26.8 4.5 %collective-permute-start.7 = (f32[2,512]{1,0:T(2,128)S(1)}, f32[2,512]{1,0:T(2,128)S(1)}, u32[]{:S(2)}, u32[]{:S(2)}) collective-permute-start(f32[2,512]{1,0:T(2,128)S(1)} %pad_maximum_fusion.1), channel_id=1, source_target_pairs={{0,2},{2,0},{1,3},{3,1},{4,6},{6,4},{5,7},{7,5},{8,10},{10,8},{9,1... | collective-permute-start | bytes 12296 | tf_op jit(solution)/shard_map/ppermute | solution.py:36
  29.3 6.7 %collective-permute-start.5 = (bf16[128,1024]{1,0:T(8,128)(2,1)S(1)}, bf16[128,1024]{1,0:T(8,128)(2,1)S(1)}, u32[]{:S(2)}, u32[]{:S(2)}) collective-permute-start(bf16[128,1024]{1,0:T(8,128)(2,1)S(1)} %collective-permute-done.2.rest_2_), channel_id=1, source_target_pairs={{0,8},{4,12},{8,16},{12,20},{16,24},{20,28},{24,0},{28,4},{1,9},{5... | collective-permute-start | bytes 786440 | tf_op jit(solution)/shard_map/ppermute | solution.py:40
  29.8 6.4 %collective-permute-start.6 = (bf16[128,1024]{1,0:T(8,128)(2,1)S(1)}, bf16[128,1024]{1,0:T(8,128)(2,1)S(1)}, u32[]{:S(2)}, u32[]{:S(2)}) collective-permute-start(bf16[128,1024]{1,0:T(8,128)(2,1)S(1)} %collective-permute-done.2.rest_2_), channel_id=1, source_target_pairs={{0,4},{4,0},{8,12},{12,8},{16,20},{20,16},{24,28},{28,24},{1,5},{5... | collective-permute-start | bytes 786440 | tf_op jit(solution)/shard_map/ppermute | solution.py:48
  36.2 12.0 %collective-permute-start.8 = (bf16[128,1024]{1,0:T(8,128)(2,1)S(1)}, bf16[128,1024]{1,0:T(8,128)(2,1)S(1)}, u32[]{:S(2)}, u32[]{:S(2)}) collective-permute-start(bf16[128,1024]{1,0:T(8,128)(2,1)S(1)} %collective-permute-done.5.rest_4_), channel_id=1, source_target_pairs={{0,8},{4,12},{8,16},{12,20},{16,24},{20,28},{24,0},{28,4},{1,9},{5... | collective-permute-start | bytes 786440 | tf_op jit(solution)/shard_map/ppermute | solution.py:40
  38.7 9.6 %collective-permute-start.9 = (bf16[128,1024]{1,0:T(8,128)(2,1)S(1)}, bf16[128,1024]{1,0:T(8,128)(2,1)S(1)}, u32[]{:S(2)}, u32[]{:S(2)}) collective-permute-start(bf16[128,1024]{1,0:T(8,128)(2,1)S(1)} %collective-permute-done.5.rest_4_), channel_id=1, source_target_pairs={{0,4},{4,0},{8,12},{12,8},{16,20},{20,16},{24,28},{28,24},{1,5},{5... | collective-permute-start | bytes 786440 | tf_op jit(solution)/shard_map/ppermute | solution.py:48
  44.0 6.4 %collective-permute-start.10 = (bf16[128,1024]{1,0:T(8,128)(2,1)S(1)}, bf16[128,1024]{1,0:T(8,128)(2,1)S(1)}, u32[]{:S(2)}, u32[]{:S(2)}) collective-permute-start(bf16[128,1024]{1,0:T(8,128)(2,1)S(1)} %shard_map.113), channel_id=1, source_target_pairs={{0,2},{2,0},{1,3},{3,1},{4,6},{6,4},{5,7},{7,5},{8,10},{10,8},{9,1... | collective-permute-start | bytes 786440 | tf_op jit(solution)/shard_map/ppermute | solution.py:36
  44.6 22.2 %copy-start.2 = (s32[8]{0:T(128)S(1)}, s32[8]{0:T(128)}, u32[]{:S(2)}) copy-start(s32[8]{0:T(128)} %get-tuple-element.92.table_ref) | copy-start | bytes 100
  44.6 22.2 %copy-start.3 = (s32[8]{0:T(128)S(1)}, s32[8]{0:T(128)}, u32[]{:S(2)}) copy-start(s32[8]{0:T(128)} %get-tuple-element.93.rank_ref) | copy-start | bytes 100
  44.6 22.2 %copy-start.4 = (s32[8]{0:T(128)S(1)}, s32[8]{0:T(128)}, u32[]{:S(2)}) copy-start(s32[8]{0:T(128)} %get-tuple-element.94.slot_pos_ref) | copy-start | bytes 100
  50.5 6.4 %collective-permute-start.11 = (bf16[128,1024]{1,0:T(8,128)(2,1)S(1)}, bf16[128,1024]{1,0:T(8,128)(2,1)S(1)}, u32[]{:S(2)}, u32[]{:S(2)}) collective-permute-start(bf16[128,1024]{1,0:T(8,128)(2,1)S(1)} %add_convert_fusion.1.rest_0_), channel_id=1, source_target_pairs={{0,8},{4,12},{8,16},{12,20},{16,24},{20,28},{24,0},{28,4},{1,9},{5... | collective-permute-start | bytes 786440 | tf_op jit(solution)/shard_map/ppermute | solution.py:40
  53.0 6.9 %collective-permute-start.12 = (bf16[128,1024]{1,0:T(8,128)(2,1)S(1)}, bf16[128,1024]{1,0:T(8,128)(2,1)S(1)}, u32[]{:S(2)}, u32[]{:S(2)}) collective-permute-start(bf16[128,1024]{1,0:T(8,128)(2,1)S(1)} %add_convert_fusion.1.rest_0_), channel_id=1, source_target_pairs={{0,4},{4,0},{8,12},{12,8},{16,20},{20,16},{24,28},{28,24},{1,5},{5... | collective-permute-start | bytes 786440 | tf_op jit(solution)/shard_map/ppermute | solution.py:48
  53.3 9.4 %collective-permute-start.13 = (bf16[128,1024]{1,0:T(8,128)(2,1)S(1)}, bf16[128,1024]{1,0:T(8,128)(2,1)S(1)}, u32[]{:S(2)}, u32[]{:S(2)}) collective-permute-start(bf16[128,1024]{1,0:T(8,128)(2,1)S(1)} %collective-permute-done.8.rest_6_), channel_id=1, source_target_pairs={{0,4},{4,0},{8,12},{12,8},{16,20},{20,16},{24,28},{28,24},{1,5},{5... | collective-permute-start | bytes 786440 | tf_op jit(solution)/shard_map/ppermute | solution.py:48
  62.7 4.1 %copy-start.8 = (bf16[128,1024]{1,0:T(8,128)(2,1)}, bf16[128,1024]{1,0:T(8,128)(2,1)S(1)}, u32[]{:S(2)}) copy-start(bf16[128,1024]{1,0:T(8,128)(2,1)S(1)} %collective-permute-done.13.rest_7_) | copy-start | bytes 786436
  62.7 10.7 %collective-permute-start.14 = (bf16[128,1024]{1,0:T(8,128)(2,1)S(1)}, bf16[128,1024]{1,0:T(8,128)(2,1)S(1)}, u32[]{:S(2)}, u32[]{:S(2)}) collective-permute-start(bf16[128,1024]{1,0:T(8,128)(2,1)S(1)} %collective-permute-done.11.rest_2_), channel_id=1, source_target_pairs={{0,8},{4,12},{8,16},{12,20},{16,24},{20,28},{24,0},{28,4},{1,9},{5... | collective-permute-start | bytes 786440 | tf_op jit(solution)/shard_map/ppermute | solution.py:40
  66.8 8.8 %collective-permute-start.15 = (bf16[128,1024]{1,0:T(8,128)(2,1)S(1)}, bf16[128,1024]{1,0:T(8,128)(2,1)S(1)}, u32[]{:S(2)}, u32[]{:S(2)}) collective-permute-start(bf16[128,1024]{1,0:T(8,128)(2,1)S(1)} %collective-permute-done.11.rest_2_), channel_id=1, source_target_pairs={{0,4},{4,0},{8,12},{12,8},{16,20},{20,16},{24,28},{28,24},{1,5},{5... | collective-permute-start | bytes 786440 | tf_op jit(solution)/shard_map/ppermute | solution.py:48
  75.6 6.4 %collective-permute-start.16 = (bf16[128,1024]{1,0:T(8,128)(2,1)S(1)}, bf16[128,1024]{1,0:T(8,128)(2,1)S(1)}, u32[]{:S(2)}, u32[]{:S(2)}) collective-permute-start(bf16[128,1024]{1,0:T(8,128)(2,1)S(1)} %collective-permute-done.14.rest_4_), channel_id=1, source_target_pairs={{0,8},{4,12},{8,16},{12,20},{16,24},{20,28},{24,0},{28,4},{1,9},{5... | collective-permute-start | bytes 786440 | tf_op jit(solution)/shard_map/ppermute | solution.py:40
  76.0 7.7 %collective-permute-start.17 = (bf16[128,1024]{1,0:T(8,128)(2,1)S(1)}, bf16[128,1024]{1,0:T(8,128)(2,1)S(1)}, u32[]{:S(2)}, u32[]{:S(2)}) collective-permute-start(bf16[128,1024]{1,0:T(8,128)(2,1)S(1)} %collective-permute-done.14.rest_4_), channel_id=1, source_target_pairs={{0,4},{4,0},{8,12},{12,8},{16,20},{20,16},{24,28},{28,24},{1,5},{5... | collective-permute-start | bytes 786440 | tf_op jit(solution)/shard_map/ppermute | solution.py:48
  82.0 6.9 %copy-start.11 = (bf16[128,1024]{1,0:T(8,128)(2,1)}, bf16[128,1024]{1,0:T(8,128)(2,1)S(1)}, u32[]{:S(2)}) copy-start(bf16[128,1024]{1,0:T(8,128)(2,1)S(1)} %collective-permute-done.16.rest_6_) | copy-start | bytes 786436
  83.7 5.2 %copy-start.12 = (bf16[128,1024]{1,0:T(8,128)(2,1)}, bf16[128,1024]{1,0:T(8,128)(2,1)S(1)}, u32[]{:S(2)}) copy-start(bf16[128,1024]{1,0:T(8,128)(2,1)S(1)} %collective-permute-done.17.rest_5_) | copy-start | bytes 786436
  83.7 9.9 %collective-permute-start.18 = (bf16[128,1024]{1,0:T(8,128)(2,1)S(1)}, bf16[128,1024]{1,0:T(8,128)(2,1)S(1)}, u32[]{:S(2)}, u32[]{:S(2)}) collective-permute-start(bf16[128,1024]{1,0:T(8,128)(2,1)S(1)} %collective-permute-done.16.rest_6_), channel_id=1, source_target_pairs={{0,4},{4,0},{8,12},{12,8},{16,20},{20,16},{24,28},{28,24},{1,5},{5... | collective-permute-start | bytes 786440 | tf_op jit(solution)/shard_map/ppermute | solution.py:48
  88.9 5.4 %copy-start.5 = (s32[8]{0:T(128)S(1)}, s32[8]{0:T(128)}, u32[]{:S(2)}) copy-start(s32[8]{0:T(128)} %slot_pos_ref.1) | copy-start | bytes 100
  88.9 5.4 %copy-start.6 = (s32[8]{0:T(128)S(1)}, s32[8]{0:T(128)}, u32[]{:S(2)}) copy-start(s32[8]{0:T(128)} %get-tuple-element.68.table_ref) | copy-start | bytes 100
  88.9 5.4 %copy-start.7 = (s32[8]{0:T(128)S(1)}, s32[8]{0:T(128)}, u32[]{:S(2)}) copy-start(s32[8]{0:T(128)} %get-tuple-element.69.rank_ref) | copy-start | bytes 100
  (1 other events, 0.7 us)
